TPU v7x, 32 devices: a whole 2x2x4 slice. The times are simulated.
32 devices in a mesh: src: 16 (over z, x, core), tm: 2 (over y).
Axes of the slice: x: 2, y: 2, z: 4, core: 2. Of those that a mesh axis runs over, the one named last changes fastest.
Arguments:
- left_vector: float32 [2, 8192], P(None, ('src', 'tm')), may hold values from -12 to 12
- source_coeffs: float32 [5, 2, 8192], P(None, None, ('src', 'tm')), may hold values from -1.5 to 1.5
- knot_coeffs: float32 [12, 2, 8192], P(None, None, ('src', 'tm')), may hold values from -1.5 to 1.5
- source_index: int32 [2, 8192], P(None, ('src', 'tm')), may hold values from 0 to 1023
- band_start: int32 [2, 8192], P(None, ('src', 'tm')), may hold values from 0 to 1023, as said below
- bucket_fill: int32 [2, 32], P(None, ('src', 'tm')), may hold values from 51 to 256, as said below
- source_vector: float32 [5, 32768], P(None, ('src', 'tm')), may hold values from -6 to 6
- knot_vector: float32 [3, 2, 4096], P(None, 'tm', 'src'), may hold values from -6 to 6
- source_search: float32 [5, 32768], P(None, ('src', 'tm')), may hold values from -6 to 6
- knot_search: float32 [3, 2, 4096], P(None, 'tm', 'src'), may hold values from -6 to 6
- source_solution: float32 [5, 32768], P(None, ('src', 'tm')), may hold values from -6 to 6
- knot_solution: float32 [3, 2, 4096], P(None, 'tm', 'src'), may hold values from -6 to 6
- recurrence: float32 [3], replicated, may hold values from 0.5 to 1.5
Outputs:
- left_next: float32 [2, 8192], P(None, ('src', 'tm'))
- source_next: float32 [5, 32768], P(None, ('src', 'tm'))
- knot_next: float32 [3, 2, 4096], P(None, 'tm', 'src')
- search_source: float32 [5, 32768], P(None, ('src', 'tm'))
- search_knot: float32 [3, 2, 4096], P(None, 'tm', 'src')
- solution_source: float32 [5, 32768], P(None, ('src', 'tm'))
- solution_knot: float32 [3, 2, 4096], P(None, 'tm', 'src')
- recurrence_next: float32 [4], replicated
Inputs may be any that keep to these rules, and one draw needn't show every extreme that they name: `bucket_fill`: in every draw one bucket of some group block holds exactly 256 observations. Call band_start // 64 the knot owner of a slot. Among the 2 x 256 slots of one column block of 256, each knot owner is named at most 64 times, and in every block some owner exactly 64 times.
All inputs are finite; a program needn't handle non-finite values.
Results may differ from a plain program's by a relative error of at most 0.00002.
Values sent between devices are 32-bit elements; how exact they have to be, the bound alone decides.
No kernel may reach another device: no remote copies, remote signals or barrier semaphores. Data moves between devices by JAX's collectives and lax.ppermute only.
A program may use at most 64 MiB of HBM per device.

v0:
```python
import jax
import jax.numpy as jnp
from jax import lax
from jax.sharding import PartitionSpec as P

KB = 4


EPSILON = 1e-06


def band_positions(band_start, knots_slab):
    rows = jnp.arange(3 * KB, dtype=jnp.int32)
    base = rows // KB * knots_slab + rows % KB
    return base[:, None, None] + KB * band_start[None]


def shards(
    left_vector,
    source_coeffs,
    knot_coeffs,
    source_index,
    band_start,
    bucket_fill,
    source_vector,
    knot_vector,
    source_search,
    knot_search,
    source_solution,
    knot_solution,
    recurrence,
):
    slab_count = lax.axis_size("tm")
    group_count = lax.axis_size("src")
    devices = slab_count * group_count
    buckets, capacity = left_vector.shape
    source_dev = source_vector.shape[1]
    knot_dev = knot_vector.shape[2]
    knots_slab = knot_dev * group_count
    total_obs = buckets * capacity * devices
    unknowns = (5 * source_dev + 3 * knot_dev) * devices
    ratio = unknowns / total_obs
    alpha = recurrence[0]
    pivot = recurrence[1]
    remainder = recurrence[2]
    slot = lax.broadcasted_iota(jnp.int32, (buckets, capacity), 1)
    valid = (slot < bucket_fill).astype(jnp.float32)
    flat_source = source_index.reshape(-1)
    picked = jnp.take(source_vector, flat_source, axis=1).reshape(5, buckets, capacity)
    image = jnp.sum(source_coeffs * picked, axis=0)
    own_knots = knot_vector[:, 0, :]
    slab_whole = lax.all_gather(own_knots, "src", axis=1, tiled=True).reshape(-1)
    positions = band_positions(band_start, knots_slab)
    knot_image = jnp.sum(knot_coeffs * jnp.take(slab_whole, positions), axis=0)
    returned = lax.all_to_all(knot_image, "tm", split_axis=0, concat_axis=0, tiled=True)
    raw = valid * (image + returned - alpha * left_vector)
    own_squares = jnp.sum(raw * raw)
    arrived = lax.all_to_all(raw, "tm", split_axis=0, concat_axis=0, tiled=True)
    gradient_source = (
        jnp.zeros((5, source_dev), jnp.float32)
        .at[:, flat_source]
        .add((source_coeffs * raw[None]).reshape(5, -1))
    )
    knot_terms = (
        jnp.zeros((3 * knots_slab,), jnp.float32)
        .at[positions.reshape(-1)]
        .add((knot_coeffs * arrived[None]).reshape(-1))
        .reshape(3, knots_slab)
    )
    knot_totals = lax.psum(knot_terms, "src")
    gradient_knot = lax.dynamic_slice_in_dim(
        knot_totals, lax.axis_index("src") * knot_dev, knot_dev, 1
    )
    gradient_squares = jnp.sum(gradient_source * gradient_source) + jnp.sum(
        gradient_knot * gradient_knot
    )
    cross = jnp.sum(gradient_source * source_vector) + jnp.sum(gradient_knot * own_knots)
    old_squares = jnp.sum(source_vector * source_vector) + jnp.sum(own_knots * own_knots)
    norm_sums = lax.psum((own_squares, gradient_squares, cross, old_squares), ("src", "tm"))
    beta = jnp.sqrt(norm_sums[0] / total_obs + EPSILON)
    scaled = ratio / beta
    source_raw = scaled * gradient_source - beta * source_vector
    knot_raw = scaled * gradient_knot - beta * own_knots
    alpha_square = (
        scaled * scaled * norm_sums[1] - 2.0 * ratio * norm_sums[2] + beta * beta * norm_sums[3]
    )
    alpha_next = jnp.sqrt(alpha_square / unknowns + EPSILON)
    left_next = raw / beta
    source_next = source_raw / alpha_next
    knot_next = knot_raw / alpha_next
    radius = jnp.sqrt(pivot * pivot + beta * beta)
    cosine = pivot / radius
    sine = beta / radius
    coupling = sine * alpha_next
    step_gain = cosine * remainder
    solution_source = source_solution + step_gain / radius * source_search
    solution_knot = knot_solution + step_gain / radius * knot_search
    search_source = source_next - coupling / radius * source_search
    search_knot = knot_next[:, None, :] - coupling / radius * knot_search
    recurrence_next = jnp.stack([alpha_next, beta, -cosine * alpha_next, sine * remainder])
    return (
        left_next,
        source_next,
        knot_next[:, None, :],
        search_source,
        search_knot,
        solution_source,
        solution_knot,
        recurrence_next,
    )


def solution(mesh):
    in_specs = (
        P(None, ("src", "tm")),
        P(None, None, ("src", "tm")),
        P(None, None, ("src", "tm")),
        P(None, ("src", "tm")),
        P(None, ("src", "tm")),
        P(None, ("src", "tm")),
        P(None, ("src", "tm")),
        P(None, "tm", "src"),
        P(None, ("src", "tm")),
        P(None, "tm", "src"),
        P(None, ("src", "tm")),
        P(None, "tm", "src"),
        P(),
    )
    out_specs = (
        P(None, ("src", "tm")),
        P(None, ("src", "tm")),
        P(None, "tm", "src"),
        P(None, ("src", "tm")),
        P(None, "tm", "src"),
        P(None, ("src", "tm")),
        P(None, "tm", "src"),
        P(),
    )
    return jax.shard_map(shards, mesh=mesh, in_specs=in_specs, out_specs=out_specs, check_vma=False)
```

profile of v0, /device:TPU:0, one launch (start us, length us, event | category | flops | bytes accessed | tf_op | source)
XLA Modules:
  0.0 217.9 jit_solution(6217080422649008223)
XLA Ops:
  0.6 0.0 copy-start.11
  0.7 23.4 %all-gather = f32[3,1,4096]{2,1,0:T(1,128)S(1)} all-gather(f32[3,1,256]{2,1,0:T(1,128)} %param.20), channel_id=2, replica_groups=mesh['src'=16,'tm'=2] {'src'}, dimensions={2}, use_global_device_ids=true | all-gather | bytes 52224 | tf_op jit(solution)/shard_map/all_gather | solution.py:52
  24.1 0.0 copy-done.11
  24.1 0.1 fusion.3
  24.2 34.3 %gather_fusion.1 = f32[6144]{0:T(1024)S(1)} fusion(f32[12288]{0:T(1024)S(1)} %bitcast.51, s32[6144]{0:T(1024)S(1)} %broadcast_clamp_fusion), kind=kCustom, calls=%fused_computation.1 | custom fusion | bytes 73728 | tf_op jit(solution)/shard_map/jit(_take)/gather | solution.py:54
  58.5 0.0 copy-start.1
  58.6 0.7 copy-done.1
  59.3 0.0 copy-start
  59.3 0.1 fusion.6
  59.4 0.6 all_to_all.14
  60.0 3.2 %all-to-all-start = ((f32[2,1,256]{2,1,0:T(1,128)}), f32[2,1,256]{2,1,0:T(1,128)S(1)}, u32[]{:S(2)}, u32[]{:S(2)}) async-start(f32[2,1,256]{2,1,0:T(1,128)} %all_to_all.14), calls=%async_computation | async-start | bytes 4096 | tf_op jit(solution)/shard_map/all_to_all | solution.py:55
  63.2 0.1 broadcast_add_fusion
  63.3 0.0 copy-done
  63.3 0.2 copy.55
  63.5 0.0 copy-start.6
  63.5 0.7 multiply_reduce_fusion.2
  64.2 0.0 copy-done.6
  64.3 1.0 gather_fusion
  65.3 0.0 copy-start.7
  65.3 0.1 copy.56
  65.5 0.0 copy-start.2
  65.5 0.7 copy-done.2
  66.2 0.0 copy-done.7
  66.2 0.6 fusion.14
  68.1 0.0 all-to-all-done
  68.1 0.0 copy-start.10
  68.1 0.0 copy-start.12
  68.1 0.7 copy-done.10
  68.8 0.0 copy-done.12
  68.8 1.3 multiply_reduce_fusion.5
  70.1 0.1 copy.61
  70.3 0.6 copy.59
  70.9 3.3 %all-to-all-start.1 = ((f32[2,1,256]{2,1,0:T(1,128)}), f32[2,1,256]{2,1,0:T(1,128)S(1)}, u32[]{:S(2)}, u32[]{:S(2)}) async-start(f32[2,1,256]{2,1,0:T(1,128)} %copy.59), calls=%async_computation.1 | async-start | bytes 4096 | tf_op jit(solution)/shard_map/all_to_all | solution.py:58
  74.1 2.4 %scatter_custom_fusion = f32[5,1024]{0,1:T(8,128)S(1)} fusion(s32[512]{0:T(512)S(1)} %bitcast.59, f32[512,5]{1,0:T(8,128)S(1)} %bitcast.53, f32[]{:T(128)} %constant.77.clone.1), kind=kCustom, calls=%fused_computation.6 | custom fusion | flops 2560 | bytes 20484 | tf_op jit(solution)/shard_map/scatter-add | solution.py:62
  76.5 0.8 multiply_reduce_fusion
  77.3 0.2 copy.58
  77.5 0.4 all-to-all-done.1
  77.9 32.5 %scatter_custom_fusion.1 = f32[12288]{0:T(1024)S(1)} fusion(s32[6144]{0:T(1024)S(1)} %bitcast.56, f32[6144]{0:T(1024)S(1)} %bitcast.57, f32[]{:T(128)} %constant.77.clone.1), kind=kCustom, calls=%fused_computation.19 | custom fusion | flops 6144 | bytes 49156 | tf_op jit(solution)/shard_map/scatter-add | solution.py:67
  110.5 0.0 copy-start.8
  110.5 0.0 copy-start.9
  110.6 0.0 copy-start.5
  110.6 57.7 %psum.36 = f32[3,4096]{1,0:T(4,128)S(1)} all-reduce(f32[3,4096]{1,0:T(4,128)S(1)} %reshape.152), channel_id=1, replica_groups=mesh['src'=16,'tm'=2] {'src'}, use_global_device_ids=true, to_apply=%region_7.8 | all-reduce | flops 12288 | bytes 98304 | tf_op jit(solution)/shard_map/psum | solution.py:70
  168.2 0.0 copy-done.5
  168.2 0.6 fusion.9
  172.8 37.2 %all-reduce = (f32[]{:T(128)}, f32[]{:T(128)}, f32[]{:T(128)}, f32[]{:T(128)}) all-reduce(f32[]{:T(128)} %get-tuple-element.43, f32[]{:T(128)S(6)} %add.192, f32[]{:T(128)S(6)} %add.193, f32[]{:T(128)S(6)} %add.194), channel_id=1, replica_groups=mesh['src'=16,'tm'=2] {'src','tm'}, use_global_device_ids=true, to_apply=%region_3.4 | all-reduce | flops 4 | bytes 32 | tf_op jit(solution)/shard_map/psum | solution.py:79
  210.7 0.6 broadcast_divide_fusion
  213.4 0.0 copy-start.4
  214.0 0.0 copy-start.3
  215.5 0.6 broadcast_in_dim.37
  216.1 0.0 copy-done.8
  216.1 0.0 copy-done.9
  216.1 0.6 multiply_add_fusion.1
  216.7 0.0 copy-done.4
  216.7 0.0 copy-done.3
  216.7 0.6 multiply_subtract_fusion
  217.3 0.6 pad_maximum_fusion
  (18 shorter events, 0.2 us)
Async XLA Ops:
  0.6 23.5 %copy-start.11 = (s32[2,256]{1,0:T(2,128)S(1)}, s32[2,256]{1,0:T(2,128)}, u32[]{:S(2)}) copy-start(s32[2,256]{1,0:T(2,128)} %param.17) | copy-start | bytes 6148
  58.5 0.7 copy-start.1
  59.3 4.0 %copy-start = (f32[5,1024]{1,0:T(8,128)S(1)}, f32[5,1024]{1,0:T(8,128)}, u32[]{:S(2)}) copy-start(f32[5,1024]{1,0:T(8,128)} %param.19) | copy-start | bytes 61444
  60.0 8.1 %all-to-all-start = ((f32[2,1,256]{2,1,0:T(1,128)}), f32[2,1,256]{2,1,0:T(1,128)S(1)}, u32[]{:S(2)}, u32[]{:S(2)}) async-start(f32[2,1,256]{2,1,0:T(1,128)} %all_to_all.14), calls=%async_computation | async-start | bytes 4096 | tf_op jit(solution)/shard_map/all_to_all | solution.py:55
  63.5 0.7 copy-start.6
  65.3 0.9 copy-start.7
  65.5 0.7 copy-start.2
  68.1 0.7 copy-start.10
  68.1 0.7 copy-start.12
  70.9 7.0 %all-to-all-start.1 = ((f32[2,1,256]{2,1,0:T(1,128)}), f32[2,1,256]{2,1,0:T(1,128)S(1)}, u32[]{:S(2)}, u32[]{:S(2)}) async-start(f32[2,1,256]{2,1,0:T(1,128)} %copy.59), calls=%async_computation.1 | async-start | bytes 4096 | tf_op jit(solution)/shard_map/all_to_all | solution.py:58
  110.5 105.6 %copy-start.8 = (f32[3,1,256]{2,1,0:T(1,128)S(1)}, f32[3,1,256]{2,1,0:T(1,128)}, u32[]{:S(2)}) copy-start(f32[3,1,256]{2,1,0:T(1,128)} %param.24) | copy-start | bytes 9220
  110.5 105.6 %copy-start.9 = (f32[3,1,256]{2,1,0:T(1,128)S(1)}, f32[3,1,256]{2,1,0:T(1,128)}, u32[]{:S(2)}) copy-start(f32[3,1,256]{2,1,0:T(1,128)} %param.22) | copy-start | bytes 9220
  110.6 57.7 %copy-start.5 = (f32[3,1,256]{2,1,0:T(1,128)S(1)}, f32[3,1,256]{2,1,0:T(1,128)}, u32[]{:S(2)}) copy-start(f32[3,1,256]{2,1,0:T(1,128)} %param.20) | copy-start | bytes 9220
  213.4 3.3 %copy-start.4 = (f32[5,1024]{1,0:T(8,128)S(1)}, f32[5,1024]{1,0:T(8,128)}, u32[]{:S(2)}) copy-start(f32[5,1024]{1,0:T(8,128)} %param.23) | copy-start | bytes 61444
  214.0 2.6 %copy-start.3 = (f32[5,1024]{1,0:T(8,128)S(1)}, f32[5,1024]{1,0:T(8,128)}, u32[]{:S(2)}) copy-start(f32[5,1024]{1,0:T(8,128)} %param.21) | copy-start | bytes 61444
where the time goes:
time: 219 us; the launch traced here: 218 us
  blocking collectives  118 us (54%)
  other arithmetic  41.1 us (19%)
  local copies, waits for them, and re-layouts  40.5 us (18%)
  between operations  11 us (5%)
  starting transfers between devices  6.49 us (3%)
    psum x1, blocking collectives, shards(): knot_totals = lax.psum(knot_terms, 'src')  57.7 us
    psum x1, blocking collectives, shards(): lax.psum((own_squares, gradient_squares, cross, old_squares), ('src', 'tm'))  37.2 us
    gather x2, local copies, waits for them, and re-layouts, shards(): knot_image = jnp.sum(knot_coeffs * jnp.take(slab_whole, positions), axis=0)  34.3 us
    scatter-add x1, other arithmetic, shards(): knot_terms = jnp.zeros((3 * knots_slab,), jnp.float32).at[positions.resha...  32.5 us
    all_gather x1, blocking collectives, shards(): lax.all_gather(own_knots, 'src', axis=1, tiled=True).reshape(-1)  23.4 us
  transfers between devices with their start and end apart: 2, of which 1 were waited for; matrix products, arithmetic and copies ran while one was open for 3% of the time, Pallas kernels for 0%

commit v1 on v0

v1 whole, which is shorter than its diff:
```python
import functools

import jax
import jax.numpy as jnp
from jax import lax
from jax.experimental import pallas as pl
from jax.experimental.pallas import tpu as pltpu
from jax.sharding import PartitionSpec as P

KB = 4
ROWS = 3 * KB
LANES = 128
EPSILON = 1e-06
F32 = jnp.float32
BF16 = jnp.bfloat16
I32 = jnp.int32


def iota(shape, axis):
    return lax.broadcasted_iota(I32, shape, axis)


def split3(x):
    hi = x.astype(BF16).astype(F32)
    rest = x - hi
    mid = rest.astype(BF16).astype(F32)
    return jnp.concatenate([hi, mid, rest - mid], axis=0).astype(BF16)


def fold3(y):
    n = y.shape[0] // 3
    return (y[2 * n :] + y[n : 2 * n]) + y[:n]


def dot(a, b):
    return lax.dot_general(a, b, (((1,), (0,)), ((), ())), preferred_element_type=F32)


def dot_nt(a, b):
    return lax.dot_general(a, b, (((1,), (1,)), ((), ())), preferred_element_type=F32)


def pick(values, onehot):
    return fold3(dot(split3(values), onehot))


def put(values, onehot):
    return fold3(dot_nt(split3(values), onehot))


def onehot(count, index):
    hit = iota((count, index.shape[1]), 0) == index
    return jnp.where(hit, 1.0, 0.0).astype(BF16)


def pad_rows(x, n):
    return jnp.concatenate([x, jnp.zeros((n - x.shape[0], x.shape[1]), F32)], axis=0)


def row_parts(shape):
    row = iota(shape, 0)
    upper = (row >= 8).astype(I32)
    held = (row - 8 * upper) < ROWS // 2
    c = row - 2 * upper
    return held, c >> 2, c & (KB - 1)


def halves(x, low):
    return jnp.where(low, x[:8], x[8:])


def before_kernel(groups, slabs, source_index, source_coeffs, source_vector, left, fill, recurrence, knot_coeffs, band, knots, send, partial_out, own):
    buckets, capacity = left.shape
    source_dev = source_vector.shape[1]
    knot_dev = knots.shape[2]
    bands = knot_dev // KB
    shift = bands.bit_length() - 1
    alpha = recurrence[0]
    low8 = iota((8, LANES), 1) < bands
    slot = iota((1, capacity), 1)

    vector = split3(pad_rows(source_vector[...], 8))
    partial = []
    for t in range(buckets):
        hot = onehot(source_dev, source_index[pl.ds(t, 1), :])
        picked = fold3(dot(vector, hot))[:5]
        image = jnp.sum(source_coeffs[:, t, :] * picked, axis=0, keepdims=True)
        partial.append(jnp.where(slot < fill[t, 0], image - alpha * left[pl.ds(t, 1), :], 0.0))
        partial_out[pl.ds(t, 1), :] = partial[t]

    total = jnp.zeros((groups, 1), F32)
    before = jnp.where(iota((capacity, capacity), 0) < iota((capacity, capacity), 1), 1.0, 0.0).astype(BF16)
    packed = jnp.zeros((16, groups * bands), F32)
    for i in range(buckets):
        bands_i = band[pl.ds(i, 1), :]
        owner = bands_i >> shift
        named = jnp.where(iota((groups, capacity), 0) == owner, 1.0, 0.0)
        count = dot(named.astype(BF16), before) + total
        rank = jnp.sum(named * count, axis=0, keepdims=True).astype(I32)
        total = total + jnp.sum(named, axis=1, keepdims=True)
        hot = onehot(groups * bands, owner * bands + rank)
        local = (bands_i - owner * bands).astype(F32)
        place = (slot + i * capacity).astype(F32)
        zero = jnp.zeros((1, capacity), F32)
        coeffs = knot_coeffs[:, i, :]
        values = jnp.concatenate([coeffs[: ROWS // 2], local, zero, coeffs[ROWS // 2 :], place, zero], axis=0)
        packed = packed + put(values, hot)

    held, axis_of, offset = row_parts((16, knot_dev))
    spread = jnp.zeros((16, knot_dev), F32)
    for a in range(3):
        spread = jnp.where(axis_of == a, knots[a], spread)
    spread = jnp.where(held & ((iota((16, knot_dev), 1) & (KB - 1)) == offset), spread, 0.0)
    hit = (iota((knot_dev, LANES), 0) >> 2) == (iota((knot_dev, LANES), 1) & (bands - 1))
    rows = pick(spread, jnp.where(hit, 1.0, 0.0).astype(BF16))
    own[...] = rows
    knot_rows = halves(rows, low8)[: ROWS // 2]

    last = iota((8, LANES), 0) == 7
    first = [
        jnp.concatenate([knot_rows] + [partial[t][:, k * LANES : (k + 1) * LANES] for k in range(2)], axis=0)
        for t in range(buckets)
    ]
    for g in range(groups // 2):
        tile = packed[:, g * LANES : (g + 1) * LANES]
        turned = pltpu.roll(tile, bands, 1)
        pair = (jnp.where(low8, tile[:8], turned[8:]), jnp.where(low8, turned[:8], tile[8:]))
        for h in range(2):
            for t in range(slabs):
                block = (2 * g + h) * slabs + t
                send[block, 0:8, :] = first[t]
                send[block, 8:16, :] = jnp.where(last, fill[t, 0].astype(F32), pair[h])


def joined(even, odd, low, bands):
    return jnp.concatenate(
        [jnp.where(low, even, pltpu.roll(odd, bands, 1)), jnp.where(low, pltpu.roll(even, bands, 1), odd)], axis=0
    )


def middle_kernel(groups, slabs, recv, exchanged, partial, left, fill, recurrence, source_index, source_coeffs, source_vector, knots, own, raw_out, gradient_source, gradient_knot, sums):
    buckets, capacity = left.shape
    source_dev = source_vector.shape[1]
    knot_dev = knots.shape[2]
    bands = knot_dev // KB
    shift = bands.bit_length() - 1
    capacity_shift = capacity.bit_length() - 1
    devices = groups * slabs
    packets = groups * bands
    alpha = recurrence[0]
    my_slab = lax.axis_index("tm")
    low = iota((8, LANES), 1) < bands
    slot = iota((1, capacity), 1)

    gathered_sum = jnp.zeros((8, source_dev), F32)
    squares = jnp.zeros((1, capacity), F32)
    cross = jnp.zeros((1, capacity), F32)
    for t in range(buckets):
        table = jnp.concatenate(
            [
                joined(recv[2 * g * slabs + t, 0:8, :], recv[(2 * g + 1) * slabs + t, 0:8, :], low, bands)
                for g in range(groups // 2)
            ],
            axis=1,
        )
        block = exchanged[t]
        coeffs = jnp.concatenate(
            [pad_rows(block[: ROWS // 2], 8), pad_rows(block[ROWS // 2 : ROWS], 8)], axis=0
        )
        hot = onehot(packets, block[ROWS : ROWS + 1].astype(I32))
        image = jnp.sum(coeffs * pick(table, hot), axis=0, keepdims=True)
        raw = partial[pl.ds(t, 1), :] + jnp.where(slot < fill[t, 0], image, 0.0)
        raw_out[pl.ds(t, 1), :] = raw
        squares = squares + raw * raw
        cross = cross + raw * (raw + alpha * left[pl.ds(t, 1), :])
        hot = onehot(source_dev, source_index[pl.ds(t, 1), :])
        gathered_sum = gathered_sum + put(pad_rows(source_coeffs[:, t, :] * raw, 8), hot)
    gradient_source[...] = gathered_sum[:5]

    packet = jnp.concatenate(
        [
            joined(
                recv[2 * g * slabs + my_slab, 8:16, :], recv[(2 * g + 1) * slabs + my_slab, 8:16, :], low, bands
            )
            for g in range(groups // 2)
        ],
        axis=1,
    )
    band = packet[6:7].astype(I32)
    place = packet[14:15].astype(I32)
    inner = place & (capacity - 1)
    sender = (iota((1, packets), 1) >> shift) * slabs + (place >> capacity_shift)
    chosen = iota((devices, packets), 0) == sender
    partials = jnp.concatenate([recv[:, 6, :], recv[:, 7, :]], axis=1)
    found = pick(partials, onehot(capacity, inner))
    fills = jnp.concatenate([recv[:, 15, :]] * (packets // LANES), axis=1)
    partial_packet = jnp.sum(jnp.where(chosen, found, 0.0), axis=0, keepdims=True)
    fill_packet = jnp.sum(jnp.where(chosen, fills, 0.0), axis=0, keepdims=True)
    hot = onehot(bands, band)
    image = jnp.sum(packet * pick(own[...][:, :bands], hot), axis=0, keepdims=True)
    raw = jnp.where(inner.astype(F32) < fill_packet, partial_packet + image, 0.0)
    collected = put(packet * raw, hot)
    hit = iota((bands, knot_dev), 0) == (iota((bands, knot_dev), 1) >> 2)
    spread = pick(collected, jnp.where(hit, 1.0, 0.0).astype(BF16))
    held, axis_of, offset = row_parts((16, knot_dev))
    spread = jnp.where(held & ((iota((16, knot_dev), 1) & (KB - 1)) == offset), spread, 0.0)
    knot_squares = jnp.zeros((1, knot_dev), F32)
    knot_old = jnp.zeros((1, knot_dev), F32)
    for a in range(3):
        total = jnp.sum(jnp.where(axis_of == a, spread, 0.0), axis=0, keepdims=True)
        gradient_knot[a] = total
        knot_squares = knot_squares + total * total
        knot_old = knot_old + knots[a] * knots[a]

    own_squares = jnp.sum(squares)
    cross_sum = jnp.sum(cross)
    gradient_squares = jnp.sum(gathered_sum * gathered_sum) + jnp.sum(knot_squares)
    old = source_vector[...]
    old_squares = jnp.sum(old * old) + jnp.sum(knot_old)
    lane = iota((devices, LANES), 1)
    sums[...] = jnp.where(
        lane == 0,
        own_squares,
        jnp.where(lane == 1, gradient_squares, jnp.where(lane == 2, cross_sum, old_squares)),
    )


def after_kernel(total_obs, unknowns, sums, recurrence, raw, gradient_source, gradient_knot, source_vector, knots, source_search, knot_search, source_solution, knot_solution, left_next, source_next, knot_next, search_source, search_knot, solution_source, solution_knot, recurrence_next):
    ratio = unknowns / total_obs
    pivot = recurrence[1]
    remainder = recurrence[2]
    total = jnp.sum(sums[...], axis=0, keepdims=True)
    s0, s1, s2, s3 = (total[:, k : k + 1] for k in range(4))
    beta = jnp.sqrt(s0 / total_obs + EPSILON)
    scaled = ratio / beta
    alpha_square = scaled * scaled * s1 - 2.0 * ratio * s2 + beta * beta * s3
    alpha_next = jnp.sqrt(alpha_square / unknowns + EPSILON)
    radius = jnp.sqrt(pivot * pivot + beta * beta)
    cosine = pivot / radius
    sine = beta / radius
    gain = cosine * remainder / radius
    turn = sine * alpha_next / radius
    one_gradient = scaled / alpha_next
    one_vector = beta / alpha_next
    left_next[...] = raw[...] / beta
    search = source_search[...]
    value = one_gradient * gradient_source[...] - one_vector * source_vector[...]
    source_next[...] = value
    search_source[...] = value - turn * search
    solution_source[...] = source_solution[...] + gain * search
    for a in range(3):
        search = knot_search[a]
        value = one_gradient * gradient_knot[a] - one_vector * knots[a]
        knot_next[a] = value
        search_knot[a] = value - turn * search
        solution_knot[a] = knot_solution[a] + gain * search
    lane = iota((1, LANES), 1)
    recurrence_next[...] = jnp.where(
        lane == 0,
        alpha_next,
        jnp.where(lane == 1, beta, jnp.where(lane == 2, -cosine * alpha_next, sine * remainder)),
    )


VMEM = pl.BlockSpec(memory_space=pltpu.VMEM)
SMEM = pl.BlockSpec(memory_space=pltpu.SMEM)


def shards(
    left_vector,
    source_coeffs,
    knot_coeffs,
    source_index,
    band_start,
    bucket_fill,
    source_vector,
    knot_vector,
    source_search,
    knot_search,
    source_solution,
    knot_solution,
    recurrence,
):
    slabs = lax.axis_size("tm")
    groups = lax.axis_size("src")
    devices = slabs * groups
    buckets, capacity = left_vector.shape
    source_dev = source_vector.shape[1]
    knot_dev = knot_vector.shape[2]
    total_obs = buckets * capacity * devices
    unknowns = (5 * source_dev + 3 * knot_dev) * devices
    params = pltpu.CompilerParams(vmem_limit_bytes=48 * 1024 * 1024)
    shape = jax.ShapeDtypeStruct

    regroup = jnp.concatenate([knot_coeffs, band_start.astype(F32)[None]], axis=0)
    regroup = jnp.transpose(regroup, (1, 0, 2))
    exchanged = lax.all_to_all(regroup, "tm", split_axis=0, concat_axis=0, tiled=True)

    send, partial, own = pl.pallas_call(
        functools.partial(before_kernel, groups, slabs),
        out_shape=(
            shape((devices, 16, LANES), F32),
            shape((buckets, capacity), F32),
            shape((16, LANES), F32),
        ),
        in_specs=[VMEM, VMEM, VMEM, VMEM, SMEM, SMEM, VMEM, VMEM, VMEM],
        out_specs=(VMEM, VMEM, VMEM),
        compiler_params=params,
        name="before",
    )(
        source_index,
        source_coeffs,
        source_vector,
        left_vector,
        bucket_fill,
        recurrence,
        knot_coeffs,
        band_start,
        knot_vector,
    )
    recv = lax.all_to_all(send, ("src", "tm"), split_axis=0, concat_axis=0, tiled=True)
    raw, gradient_source, gradient_knot, sums = pl.pallas_call(
        functools.partial(middle_kernel, groups, slabs),
        out_shape=(
            shape((buckets, capacity), F32),
            shape((5, source_dev), F32),
            shape((3, 1, knot_dev), F32),
            shape((devices, LANES), F32),
        ),
        in_specs=[VMEM, VMEM, VMEM, VMEM, SMEM, SMEM, VMEM, VMEM, VMEM, VMEM, VMEM],
        out_specs=(VMEM, VMEM, VMEM, VMEM),
        compiler_params=params,
        name="middle",
    )(
        recv,
        exchanged,
        partial,
        left_vector,
        bucket_fill,
        recurrence,
        source_index,
        source_coeffs,
        source_vector,
        knot_vector,
        own,
    )
    sums = lax.all_to_all(sums, ("src", "tm"), split_axis=0, concat_axis=0, tiled=True)
    like = [shape(x.shape, F32) for x in (left_vector, source_vector, knot_vector)]
    outs = pl.pallas_call(
        functools.partial(after_kernel, total_obs, unknowns),
        out_shape=(like[0], like[1], like[2], like[1], like[2], like[1], like[2], shape((1, LANES), F32)),
        in_specs=[VMEM, SMEM] + [VMEM] * 9,
        out_specs=(VMEM,) * 8,
        compiler_params=params,
        name="after",
    )(
        sums,
        recurrence,
        raw,
        gradient_source,
        gradient_knot,
        source_vector,
        knot_vector,
        source_search,
        knot_search,
        source_solution,
        knot_solution,
    )
    return (*outs[:7], outs[7][0, :4])


def solution(mesh):
    wide = ("src", "tm")
    flat = P(None, wide)
    knot = P(None, "tm", "src")
    in_specs = (flat, P(None, None, wide), P(None, None, wide), flat, flat, flat, flat, knot, flat, knot, flat, knot, P())
    out_specs = (flat, flat, knot, flat, knot, flat, knot, P())
    return jax.shard_map(shards, mesh=mesh, in_specs=in_specs, out_specs=out_specs, check_vma=False)
```

time: 219 us -> 40.6 us (0.19)
  blocking collectives: 118 us -> 25.2 us
  other arithmetic: 41.1 us -> 0.63 us
  local copies, waits for them, and re-layouts: 40.5 us -> 2.62 us
  between operations: 11 us -> 0.73 us
  Pallas kernels: 0 us -> 4.92 us
    psum x2 -> x0, blocking collectives: 94.9 us -> none  [the longest x1 57.7 us: shards(): knot_totals = lax.psum(knot_terms, 'src')]
    gather x4 -> x0, local copies, waits for them, and re-layouts: 35.4 us -> none  [the longest x2 34.3 us: shards(): knot_image = jnp.sum(knot_coeffs * jnp.take(slab_whole, positions), axis=0)]
    scatter-add x2 -> x0, other arithmetic: 34.9 us -> none  [the longest x1 32.5 us: shards(): knot_terms = jnp.zeros((3 * knots_slab,), jnp.float32).at[positions.resha...]
    all_to_all x0 -> x2, blocking collectives: none -> 25.2 us  [the longest x1 15.8 us: shards(): lax.all_to_all(send, ('src', 'tm'), split_axis=0, concat_axis=0, tiled=True)]
    all_gather x1 -> x0, blocking collectives: 23.4 us -> none  [shards(): lax.all_gather(own_knots, 'src', axis=1, tiled=True).reshape(-1)]
    pallas_call x0 -> x3, Pallas kernels: none -> 4.92 us  [the longest x1 2.04 us: shards(): pl.pallas_call(functools.partial(middle_kernel, groups, slabs), out_shape...]
    reduce_sum x6 -> x0, other arithmetic: 3.51 us -> none  [the longest x1 1.31 us: shards(): own_squares = jnp.sum(raw * raw)]
    all_to_all x2 -> x1, starting transfers between devices: 6.49 us -> 4.38 us  [shards(): lax.all_to_all(regroup, 'tm', split_axis=0, concat_axis=0, tiled=True)]
  transfers between devices with their start and end apart: 2 -> 1, of which waited for: 1 -> 1; matrix products, arithmetic and copies ran while one was open for 3% -> 0% of each run, Pallas kernels for 0% -> 4%
where the time goes in v1:
time: 40.6 us; the launch traced here: 40.2 us
  blocking collectives  25.2 us (62%)
  Pallas kernels  4.92 us (12%)
  starting transfers between devices  4.38 us (11%)
  local copies, waits for them, and re-layouts  2.62 us (6%)
  waiting for transfers between devices  1.74 us (4%)
  between operations  0.73 us (2%)
  other arithmetic  0.63 us (2%)
    all_to_all x1, blocking collectives, shards(): lax.all_to_all(send, ('src', 'tm'), split_axis=0, concat_axis=0, tiled=True)  15.8 us
    all_to_all x1, blocking collectives, shards(): lax.all_to_all(sums, ('src', 'tm'), split_axis=0, concat_axis=0, tiled=True)  9.32 us
    all_to_all x1, starting transfers between devices, shards(): lax.all_to_all(regroup, 'tm', split_axis=0, concat_axis=0, tiled=True)  4.38 us
    unnamed x28, local copies, waits for them, and re-layouts  2.1 us
    pallas_call x1, Pallas kernels, shards(): pl.pallas_call(functools.partial(middle_kernel, groups, slabs), out_shape...  2.04 us
    all_to_all x1, waiting for transfers between devices, shards(): lax.all_to_all(regroup, 'tm', split_axis=0, concat_axis=0, tiled=True)  1.74 us
    pallas_call x1, Pallas kernels, shards(): pl.pallas_call(functools.partial(before_kernel, groups, slabs), out_shape...  1.54 us
    pallas_call x1, Pallas kernels, shards(): pl.pallas_call(functools.partial(after_kernel, total_obs, unknowns), out_...  1.34 us
  transfers between devices with their start and end apart: 1, of which 1 were waited for; matrix products, arithmetic and copies ran while one was open for 0% of the time, Pallas kernels for 4%

profile of v1, /device:TPU:0, one launch (start us, length us, event | category | flops | bytes accessed | tf_op | source)
XLA Modules:
  0.0 40.2 jit_solution(3383921749273369868)
XLA Ops:
  0.6 0.0 copy-start.8
  0.6 0.7 %copy.25 = f32[12,2,256]{2,0,1:T(8,128)S(1)} copy(f32[12,2,256]{2,1,0:T(2,128)} %knot_coeffs.1) | data formatting | bytes 49152 | tf_op args[2]
  1.4 0.0 copy-done.8
  1.4 0.0 copy-start.2
  1.4 0.6 %maximum_bitcast_fusion = f32[2,13,256]{2,1,0:T(8,128)} fusion(f32[1,2,256]{2,0,1:T(1,128)S(1)} %broadcast_in_dim.3, f32[12,2,256]{2,0,1:T(8,128)S(1)} %copy.25), kind=kLoop, calls=%fused_computation | loop fusion | flops 6656 | bytes 53248 | tf_op jit(solution)/shard_map/transpose | solution.py:296
  2.0 0.0 copy-start.12
  2.0 0.0 copy-start
  2.0 0.0 copy-start.1
  2.0 0.0 copy-start.5
  2.0 0.0 copy-start.6
  2.1 0.0 copy-start.7
  2.1 4.4 %all-to-all-start.1 = ((f32[2,13,256]{2,1,0:T(8,128)}), f32[2,13,256]{2,1,0:T(8,128)S(1)}, u32[]{:S(2)}, u32[]{:S(2)}) async-start(f32[2,13,256]{2,1,0:T(8,128)} %maximum_bitcast_fusion), calls=%async_computation.1 | async-start | bytes 65536 | tf_op jit(solution)/shard_map/all_to_all | solution.py:297
  6.5 0.0 copy-done.12
  6.5 0.0 copy-start.9
  6.5 0.1 copy.24.fill
  6.5 0.0 copy-done.2
  6.6 0.0 copy-done
  6.6 0.0 copy-done.1
  6.6 0.0 copy-done.5
  6.6 0.0 copy-done.6
  6.6 0.0 copy-done.7
  6.6 0.5 %copy-done.9 = f32[3]{0:T(128)S(1)} copy-done((f32[3]{0:T(128)S(1)}, f32[3]{0:T(128)}, u32[]{:S(2)}) %copy-start.9) | copy-done | bytes 36
  7.1 1.5 %before.1 = (f32[32,16,128]{2,1,0:T(8,128)S(1)}, f32[2,256]{1,0:T(2,128)S(1)}, f32[16,128]{1,0:T(8,128)S(1)}) custom-call(s32[2,256]{1,0:T(2,128)S(1)} %copy-done.6, f32[5,2,256]{2,1,0:T(2,128)S(1)} %copy-done.2, f32[5,1024]{1,0:T(8,128)S(1)} %copy-done, f32[2,256]{1,0:T(2,128)S(1)} %copy-done.7, s32[2,1]{1,0:T(2,128)S(1)} %copy.24.fill, f32[3]{0:T(128)S(1)} %copy-done.9, ...), custom_call_target="tpu_custom_call" | custom-call | tf_op jit(solution)/shard_map/before/pallas_call | solution.py:299
  8.7 1.7 %all-to-all-done.1.exchanged = f32[2,13,256]{2,1,0:T(8,128)S(1)} async-done(((f32[2,13,256]{2,1,0:T(8,128)}), f32[2,13,256]{2,1,0:T(8,128)S(1)}, u32[]{:S(2)}, u32[]{:S(2)}) %all-to-all-start.1) | async-done | bytes 26656 | tf_op jit(solution)/shard_map/all_to_all | solution.py:297
  10.4 15.8 %all_to_all.21.recv = f32[32,16,128]{2,1,0:T(8,128)S(1)} all-to-all(f32[32,16,128]{2,1,0:T(8,128)S(1)} %get-tuple-element.23), channel_id=1, replica_groups=mesh['src'=16,'tm'=2] {'src','tm'}, dimensions={0} | all-to-all | bytes 524288 | tf_op jit(solution)/shard_map/all_to_all | solution.py:321
  26.2 0.0 copy-start.4
  26.2 2.0 %middle.1 = (f32[2,256]{1,0:T(2,128)S(1)}, f32[5,1024]{1,0:T(8,128)S(1)}, f32[3,1,256]{2,1,0:T(1,128)S(1)}, f32[32,128]{1,0:T(8,128)S(1)}) custom-call(f32[32,16,128]{2,1,0:T(8,128)S(1)} %all_to_all.21.recv, f32[2,13,256]{2,1,0:T(8,128)S(1)} %all-to-all-done.1.exchanged, f32[2,256]{1,0:T(2,128)S(1)} %get-tuple-element.24.partial, f32[2,256]{1,0:T(2,128)S(1)} %copy-done.7, ...), custom_call_target="tpu_custom_call" | custom-call | tf_op jit(solution)/shard_map/middle/pallas_call | solution.py:322
  28.3 0.0 copy-start.3
  28.3 9.3 %all_to_all.22 = f32[32,1,128]{2,1,0:T(1,128)S(1)} all-to-all(f32[32,1,128]{2,1,0:T(1,128)S(1)} %bitcast.9), channel_id=1, replica_groups=mesh['src'=16,'tm'=2] {'src','tm'}, dimensions={0} | all-to-all | bytes 32768 | tf_op jit(solution)/shard_map/all_to_all | solution.py:347
  37.6 0.0 copy-start.11
  37.6 0.0 copy-start.10
  37.6 0.0 copy-done.4
  37.6 0.0 copy-done.3
  37.6 0.7 %copy-done.11 = f32[3,1,256]{2,1,0:T(1,128)S(1)} copy-done((f32[3,1,256]{2,1,0:T(1,128)S(1)}, f32[3,1,256]{2,1,0:T(1,128)}, u32[]{:S(2)}) %copy-start.11) | copy-done | bytes 3096
  38.3 0.0 copy-done.10
  38.3 1.3 %after.1 = (f32[2,256]{1,0:T(2,128)}, f32[5,1024]{1,0:T(8,128)}, f32[3,1,256]{2,1,0:T(1,128)}, f32[5,1024]{1,0:T(8,128)}, f32[3,1,256]{2,1,0:T(1,128)}, /*index=...) custom-call(f32[32,128]{1,0:T(8,128)S(1)} %bitcast.8, f32[3]{0:T(128)S(1)} %copy-done.9, ...), custom_call_target="tpu_custom_call" | custom-call | tf_op jit(solution)/shard_map/after/pallas_call | solution.py:349
  39.7 0.5 %slice_bitcast_fusion = f32[4]{0:T(128)} fusion(f32[1,128]{1,0:T(1,128)S(1)} %get-tuple-element.37), kind=kLoop, calls=%fused_computation.1 | loop fusion | bytes 32 | tf_op jit(solution)/shard_map/squeeze | solution.py:369
  (2 shorter events, 0.0 us)
Async XLA Ops:
  0.6 0.8 %copy-start.8 = (s32[2,256]{1,0:T(2,128)S(1)}, s32[2,256]{1,0:T(2,128)}, u32[]{:S(2)}) copy-start(s32[2,256]{1,0:T(2,128)} %band.1) | copy-start | bytes 6148
  1.4 5.1 %copy-start.2 = (f32[5,2,256]{2,1,0:T(2,128)S(1)}, f32[5,2,256]{2,1,0:T(2,128)}, u32[]{:S(2)}) copy-start(f32[5,2,256]{2,1,0:T(2,128)} %source_coeffs.3) | copy-start | bytes 30724
  2.0 4.4 %copy-start.12 = (s32[2,1]{0,1:T(1,128)S(1)}, s32[2,1]{0,1:T(1,128)}, u32[]{:S(2)}) copy-start(s32[2,1]{0,1:T(1,128)} %param.18) | copy-start | bytes 28
  2.0 4.5 %copy-start = (f32[5,1024]{1,0:T(8,128)S(1)}, f32[5,1024]{1,0:T(8,128)}, u32[]{:S(2)}) copy-start(f32[5,1024]{1,0:T(8,128)} %source_vector.5) | copy-start | bytes 61444
  2.0 4.5 %copy-start.1 = (f32[12,2,256]{2,1,0:T(2,128)S(1)}, f32[12,2,256]{2,1,0:T(2,128)}, u32[]{:S(2)}) copy-start(f32[12,2,256]{2,1,0:T(2,128)} %knot_coeffs.1) | copy-start | bytes 73732
  2.0 4.5 %copy-start.5 = (f32[3,1,256]{2,1,0:T(1,128)S(1)}, f32[3,1,256]{2,1,0:T(1,128)}, u32[]{:S(2)}) copy-start(f32[3,1,256]{2,1,0:T(1,128)} %knots.5) | copy-start | bytes 9220
  2.0 4.5 %copy-start.6 = (s32[2,256]{1,0:T(2,128)S(1)}, s32[2,256]{1,0:T(2,128)}, u32[]{:S(2)}) copy-start(s32[2,256]{1,0:T(2,128)} %source_index.3) | copy-start | bytes 6148
  2.1 4.5 %copy-start.7 = (f32[2,256]{1,0:T(2,128)S(1)}, f32[2,256]{1,0:T(2,128)}, u32[]{:S(2)}) copy-start(f32[2,256]{1,0:T(2,128)} %left.3) | copy-start | bytes 6148
  2.1 8.3 %all-to-all-start.1 = ((f32[2,13,256]{2,1,0:T(8,128)}), f32[2,13,256]{2,1,0:T(8,128)S(1)}, u32[]{:S(2)}, u32[]{:S(2)}) async-start(f32[2,13,256]{2,1,0:T(8,128)} %maximum_bitcast_fusion), calls=%async_computation.1 | async-start | bytes 65536 | tf_op jit(solution)/shard_map/all_to_all | solution.py:297
  6.5 0.7 %copy-start.9 = (f32[3]{0:T(128)S(1)}, f32[3]{0:T(128)}, u32[]{:S(2)}) copy-start(f32[3]{0:T(128)} %recurrence.5) | copy-start | bytes 40
  26.2 11.4 %copy-start.4 = (f32[5,1024]{1,0:T(8,128)S(1)}, f32[5,1024]{1,0:T(8,128)}, u32[]{:S(2)}) copy-start(f32[5,1024]{1,0:T(8,128)} %source_solution.1) | copy-start | bytes 61444
  28.3 9.3 %copy-start.3 = (f32[5,1024]{1,0:T(8,128)S(1)}, f32[5,1024]{1,0:T(8,128)}, u32[]{:S(2)}) copy-start(f32[5,1024]{1,0:T(8,128)} %source_search.1) | copy-start | bytes 61444
  37.6 0.7 %copy-start.11 = (f32[3,1,256]{2,1,0:T(1,128)S(1)}, f32[3,1,256]{2,1,0:T(1,128)}, u32[]{:S(2)}) copy-start(f32[3,1,256]{2,1,0:T(1,128)} %knot_solution.1) | copy-start | bytes 9220
  37.6 0.7 %copy-start.10 = (f32[3,1,256]{2,1,0:T(1,128)S(1)}, f32[3,1,256]{2,1,0:T(1,128)}, u32[]{:S(2)}) copy-start(f32[3,1,256]{2,1,0:T(1,128)} %knot_search.1) | copy-start | bytes 9220

commit v2 on v1

--- a/solution.py
+++ b/solution.py
@@ -40,12 +40,31 @@
     return lax.dot_general(a, b, (((1,), (1,)), ((), ())), preferred_element_type=F32)
 
 
-def pick(values, onehot):
-    return fold3(dot(split3(values), onehot))
-
-
-def put(values, onehot):
-    return fold3(dot_nt(split3(values), onehot))
+WIDE = 256
+
+
+def pick(values, index):
+    rows, count = values.shape
+    width = min(count, WIDE)
+    parts = count // width
+    stacked = jnp.concatenate([values[:, h * width : (h + 1) * width] for h in range(parts)], axis=0)
+    found = fold3(dot(split3(stacked), onehot(width, index & (width - 1))))
+    high = index >> (width.bit_length() - 1)
+    result = found[:rows]
+    for h in range(1, parts):
+        result = jnp.where(high == h, found[h * rows : (h + 1) * rows], result)
+    return result
+
+
+def put(values, index, count):
+    rows = values.shape[0]
+    width = min(count, WIDE)
+    parts = count // width
+    high = index >> (width.bit_length() - 1)
+    if parts > 1:
+        values = jnp.concatenate([jnp.where(high == h, values, 0.0) for h in range(parts)], axis=0)
+    sums = fold3(dot_nt(split3(values), onehot(width, index & (width - 1))))
+    return jnp.concatenate([sums[h * rows : (h + 1) * rows] for h in range(parts)], axis=1)
 
 
 def onehot(count, index):
@@ -69,7 +88,20 @@
     return jnp.where(low, x[:8], x[8:])
 
 
-def before_kernel(groups, slabs, source_index, source_coeffs, source_vector, left, fill, recurrence, knot_coeffs, band, knots, send, partial_out, own):
+def fetch(sources, targets, semaphores):
+    copies = [pltpu.make_async_copy(a, b, semaphores.at[k]) for k, (a, b) in enumerate(zip(sources, targets))]
+    for copy in copies:
+        copy.start()
+    return copies
+
+
+def before_kernel(groups, slabs, *refs):
+    count = 9
+    sources, (send, partial_out, own) = refs[:count], refs[count : count + 3]
+    targets, semaphores = refs[count + 3 : -1], refs[-1]
+    for copy in fetch(sources, targets, semaphores):
+        copy.wait()
+    source_index, source_coeffs, source_vector, left, fill, recurrence, knot_coeffs, band, knots = targets
     buckets, capacity = left.shape
     source_dev = source_vector.shape[1]
     knot_dev = knots.shape[2]
@@ -79,18 +111,17 @@
     low8 = iota((8, LANES), 1) < bands
     slot = iota((1, capacity), 1)
 
-    vector = split3(pad_rows(source_vector[...], 8))
+    index = jnp.concatenate([source_index[pl.ds(t, 1), :] for t in range(buckets)], axis=1)
+    picked = pick(pad_rows(source_vector[...], 8), index)[:5]
     partial = []
     for t in range(buckets):
-        hot = onehot(source_dev, source_index[pl.ds(t, 1), :])
-        picked = fold3(dot(vector, hot))[:5]
-        image = jnp.sum(source_coeffs[:, t, :] * picked, axis=0, keepdims=True)
-        partial.append(jnp.where(slot < fill[t, 0], image - alpha * left[pl.ds(t, 1), :], 0.0))
+        image = jnp.sum(source_coeffs[:, t, :] * picked[:, t * capacity : (t + 1) * capacity], axis=0, keepdims=True)
+        partial.append(jnp.where(slot < fill[t], image - alpha * left[pl.ds(t, 1), :], 0.0))
         partial_out[pl.ds(t, 1), :] = partial[t]
 
     total = jnp.zeros((groups, 1), F32)
     before = jnp.where(iota((capacity, capacity), 0) < iota((capacity, capacity), 1), 1.0, 0.0).astype(BF16)
-    packed = jnp.zeros((16, groups * bands), F32)
+    targets, columns = [], []
     for i in range(buckets):
         bands_i = band[pl.ds(i, 1), :]
         owner = bands_i >> shift
@@ -98,13 +129,15 @@
         count = dot(named.astype(BF16), before) + total
         rank = jnp.sum(named * count, axis=0, keepdims=True).astype(I32)
         total = total + jnp.sum(named, axis=1, keepdims=True)
-        hot = onehot(groups * bands, owner * bands + rank)
+        targets.append(owner * bands + rank)
         local = (bands_i - owner * bands).astype(F32)
         place = (slot + i * capacity).astype(F32)
         zero = jnp.zeros((1, capacity), F32)
         coeffs = knot_coeffs[:, i, :]
-        values = jnp.concatenate([coeffs[: ROWS // 2], local, zero, coeffs[ROWS // 2 :], place, zero], axis=0)
-        packed = packed + put(values, hot)
+        columns.append(
+            jnp.concatenate([coeffs[: ROWS // 2], local, zero, coeffs[ROWS // 2 :], place, zero], axis=0)
+        )
+    packed = put(jnp.concatenate(columns, axis=1), jnp.concatenate(targets, axis=1), groups * bands)
 
     held, axis_of, offset = row_parts((16, knot_dev))
     spread = jnp.zeros((16, knot_dev), F32)
@@ -112,8 +145,13 @@
         spread = jnp.where(axis_of == a, knots[a], spread)
     spread = jnp.where(held & ((iota((16, knot_dev), 1) & (KB - 1)) == offset), spread, 0.0)
     hit = (iota((knot_dev, LANES), 0) >> 2) == (iota((knot_dev, LANES), 1) & (bands - 1))
-    rows = pick(spread, jnp.where(hit, 1.0, 0.0).astype(BF16))
-    own[...] = rows
+    rows = fold3(dot(split3(spread), jnp.where(hit, 1.0, 0.0).astype(BF16)))
+    own[0:16, :] = rows
+    row, lane = iota((own.shape[0] - 16, LANES), 0), iota((own.shape[0] - 16, LANES), 1)
+    scalars = jnp.where(lane == 0, alpha, jnp.where(lane == 1, recurrence[1], recurrence[2]))
+    for t in range(buckets):
+        scalars = jnp.where(row == 1 + t, fill[t].astype(F32), scalars)
+    own[16:, :] = scalars
     knot_rows = halves(rows, low8)[: ROWS // 2]
 
     last = iota((8, LANES), 0) == 7
@@ -129,7 +167,7 @@
             for t in range(slabs):
                 block = (2 * g + h) * slabs + t
                 send[block, 0:8, :] = first[t]
-                send[block, 8:16, :] = jnp.where(last, fill[t, 0].astype(F32), pair[h])
+                send[block, 8:16, :] = jnp.where(last, fill[t].astype(F32), pair[h])
 
 
 def joined(even, odd, low, bands):
@@ -138,7 +176,8 @@
     )
 
 
-def middle_kernel(groups, slabs, recv, exchanged, partial, left, fill, recurrence, source_index, source_coeffs, source_vector, knots, own, raw_out, gradient_source, gradient_knot, sums):
+def middle_kernel(groups, slabs, recv, partial, left, source_index, source_coeffs, source_vector, knots, own, *refs):
+    later_in, refs, semaphores = refs[:4], refs[4:-1], refs[-1]
     buckets, capacity = left.shape
     source_dev = source_vector.shape[1]
     knot_dev = knots.shape[2]
@@ -147,15 +186,18 @@
     capacity_shift = capacity.bit_length() - 1
     devices = groups * slabs
     packets = groups * bands
-    alpha = recurrence[0]
+    alpha = own[16:17, 0:1]
     my_slab = lax.axis_index("tm")
+    moved, (raw_out, gradient_source, gradient_knot, sums) = refs[: 2 * slabs], refs[2 * slabs : -4]
+    later = fetch(later_in, refs[-4:], semaphores)
     low = iota((8, LANES), 1) < bands
-    slot = iota((1, capacity), 1)
-
-    gathered_sum = jnp.zeros((8, source_dev), F32)
+    slot = iota((1, capacity), 1).astype(F32)
+
+    indices, weighted = [], []
     squares = jnp.zeros((1, capacity), F32)
     cross = jnp.zeros((1, capacity), F32)
-    for t in range(buckets):
+    for k in range(slabs):
+        t = lax.rem(my_slab + (slabs - k), slabs)
         table = jnp.concatenate(
             [
                 joined(recv[2 * g * slabs + t, 0:8, :], recv[(2 * g + 1) * slabs + t, 0:8, :], low, bands)
@@ -163,18 +205,19 @@
             ],
             axis=1,
         )
-        block = exchanged[t]
+        block = moved[2 * k][:, my_slab, :]
         coeffs = jnp.concatenate(
-            [pad_rows(block[: ROWS // 2], 8), pad_rows(block[ROWS // 2 : ROWS], 8)], axis=0
+            [pad_rows(block[: ROWS // 2], 8), pad_rows(block[ROWS // 2 :], 8)], axis=0
         )
-        hot = onehot(packets, block[ROWS : ROWS + 1].astype(I32))
-        image = jnp.sum(coeffs * pick(table, hot), axis=0, keepdims=True)
-        raw = partial[pl.ds(t, 1), :] + jnp.where(slot < fill[t, 0], image, 0.0)
+        found = pick(table, moved[2 * k + 1][pl.ds(my_slab, 1), :])
+        image = jnp.sum(coeffs * found, axis=0, keepdims=True)
+        raw = partial[pl.ds(t, 1), :] + jnp.where(slot < own[pl.ds(17 + t, 1), 0:1], image, 0.0)
         raw_out[pl.ds(t, 1), :] = raw
         squares = squares + raw * raw
         cross = cross + raw * (raw + alpha * left[pl.ds(t, 1), :])
-        hot = onehot(source_dev, source_index[pl.ds(t, 1), :])
-        gathered_sum = gathered_sum + put(pad_rows(source_coeffs[:, t, :] * raw, 8), hot)
+        indices.append(source_index[pl.ds(t, 1), :])
+        weighted.append(pad_rows(source_coeffs[:, t, :] * raw, 8))
+    gathered_sum = put(jnp.concatenate(weighted, axis=1), jnp.concatenate(indices, axis=1), source_dev)
     gradient_source[...] = gathered_sum[:5]
 
     packet = jnp.concatenate(
@@ -192,16 +235,15 @@
     sender = (iota((1, packets), 1) >> shift) * slabs + (place >> capacity_shift)
     chosen = iota((devices, packets), 0) == sender
     partials = jnp.concatenate([recv[:, 6, :], recv[:, 7, :]], axis=1)
-    found = pick(partials, onehot(capacity, inner))
+    found = pick(partials, inner)
     fills = jnp.concatenate([recv[:, 15, :]] * (packets // LANES), axis=1)
     partial_packet = jnp.sum(jnp.where(chosen, found, 0.0), axis=0, keepdims=True)
     fill_packet = jnp.sum(jnp.where(chosen, fills, 0.0), axis=0, keepdims=True)
-    hot = onehot(bands, band)
-    image = jnp.sum(packet * pick(own[...][:, :bands], hot), axis=0, keepdims=True)
+    image = jnp.sum(packet * pick(own[0:16, 0:bands], band), axis=0, keepdims=True)
     raw = jnp.where(inner.astype(F32) < fill_packet, partial_packet + image, 0.0)
-    collected = put(packet * raw, hot)
+    collected = put(packet * raw, band, bands)
     hit = iota((bands, knot_dev), 0) == (iota((bands, knot_dev), 1) >> 2)
-    spread = pick(collected, jnp.where(hit, 1.0, 0.0).astype(BF16))
+    spread = fold3(dot(split3(collected), jnp.where(hit, 1.0, 0.0).astype(BF16)))
     held, axis_of, offset = row_parts((16, knot_dev))
     spread = jnp.where(held & ((iota((16, knot_dev), 1) & (KB - 1)) == offset), spread, 0.0)
     knot_squares = jnp.zeros((1, knot_dev), F32)
@@ -223,12 +265,13 @@
         own_squares,
         jnp.where(lane == 1, gradient_squares, jnp.where(lane == 2, cross_sum, old_squares)),
     )
-
-
-def after_kernel(total_obs, unknowns, sums, recurrence, raw, gradient_source, gradient_knot, source_vector, knots, source_search, knot_search, source_solution, knot_solution, left_next, source_next, knot_next, search_source, search_knot, solution_source, solution_knot, recurrence_next):
+    for copy in later:
+        copy.wait()
+
+
+def after_kernel(total_obs, unknowns, sums, own, raw, gradient_source, gradient_knot, source_vector, knots, source_search, knot_search, source_solution, knot_solution, left_next, source_next, knot_next, search_source, search_knot, solution_source, solution_knot, recurrence_next):
     ratio = unknowns / total_obs
-    pivot = recurrence[1]
-    remainder = recurrence[2]
+    pivot, remainder = own[16:17, 1:2], own[16:17, 2:3]
     total = jnp.sum(sums[...], axis=0, keepdims=True)
     s0, s1, s2, s3 = (total[:, k : k + 1] for k in range(4))
     beta = jnp.sqrt(s0 / total_obs + EPSILON)
@@ -254,16 +297,13 @@
         knot_next[a] = value
         search_knot[a] = value - turn * search
         solution_knot[a] = knot_solution[a] + gain * search
-    lane = iota((1, LANES), 1)
-    recurrence_next[...] = jnp.where(
-        lane == 0,
-        alpha_next,
-        jnp.where(lane == 1, beta, jnp.where(lane == 2, -cosine * alpha_next, sine * remainder)),
-    )
+    for k, value in enumerate((alpha_next, beta, -cosine * alpha_next, sine * remainder)):
+        recurrence_next[k] = value[0, 0]
 
 
 VMEM = pl.BlockSpec(memory_space=pltpu.VMEM)
 SMEM = pl.BlockSpec(memory_space=pltpu.SMEM)
+HBM = pl.BlockSpec(memory_space=pltpu.HBM)
 
 
 def shards(
@@ -292,81 +332,87 @@
     params = pltpu.CompilerParams(vmem_limit_bytes=48 * 1024 * 1024)
     shape = jax.ShapeDtypeStruct
 
-    regroup = jnp.concatenate([knot_coeffs, band_start.astype(F32)[None]], axis=0)
-    regroup = jnp.transpose(regroup, (1, 0, 2))
-    exchanged = lax.all_to_all(regroup, "tm", split_axis=0, concat_axis=0, tiled=True)
-
-    send, partial, own = pl.pallas_call(
-        functools.partial(before_kernel, groups, slabs),
-        out_shape=(
-            shape((devices, 16, LANES), F32),
-            shape((buckets, capacity), F32),
-            shape((16, LANES), F32),
-        ),
-        in_specs=[VMEM, VMEM, VMEM, VMEM, SMEM, SMEM, VMEM, VMEM, VMEM],
-        out_specs=(VMEM, VMEM, VMEM),
-        compiler_params=params,
-        name="before",
-    )(
+    moved = []
+    for k in range(1, slabs):
+        shifted = [(t, (t + k) % slabs) for t in range(slabs)]
+        moved += [lax.ppermute(knot_coeffs, "tm", shifted), lax.ppermute(band_start, "tm", shifted)]
+
+    fill = bucket_fill.reshape(-1)
+    operands = (
         source_index,
         source_coeffs,
         source_vector,
         left_vector,
-        bucket_fill,
+        fill,
         recurrence,
         knot_coeffs,
         band_start,
         knot_vector,
     )
+    send, partial, own = pl.pallas_call(
+        functools.partial(before_kernel, groups, slabs),
+        out_shape=(
+            pltpu.VMEM((devices, 16, LANES), F32),
+            shape((buckets, capacity), F32),
+            shape((16 + 8 * pl.cdiv(1 + buckets, 8), LANES), F32),
+        ),
+        in_specs=[HBM] * len(operands),
+        out_specs=(VMEM, VMEM, VMEM),
+        scratch_shapes=[(pltpu.SMEM if x.ndim == 1 else pltpu.VMEM)(x.shape, x.dtype) for x in operands]
+        + [pltpu.SemaphoreType.DMA((len(operands),))],
+        compiler_params=params,
+        name="before",
+    )(*(pltpu.with_memory_space_constraint(x, pltpu.HBM) for x in operands))
     recv = lax.all_to_all(send, ("src", "tm"), split_axis=0, concat_axis=0, tiled=True)
-    raw, gradient_source, gradient_knot, sums = pl.pallas_call(
+    later = (source_search, knot_search, source_solution, knot_solution)
+    raw, gradient_source, gradient_knot, sums, *later = pl.pallas_call(
         functools.partial(middle_kernel, groups, slabs),
         out_shape=(
             shape((buckets, capacity), F32),
             shape((5, source_dev), F32),
             shape((3, 1, knot_dev), F32),
             shape((devices, LANES), F32),
+            *(shape(x.shape, F32) for x in later),
         ),
-        in_specs=[VMEM, VMEM, VMEM, VMEM, SMEM, SMEM, VMEM, VMEM, VMEM, VMEM, VMEM],
-        out_specs=(VMEM, VMEM, VMEM, VMEM),
+        in_specs=[VMEM] * 8 + [HBM] * 4 + [VMEM] * (2 * slabs),
+        out_specs=(VMEM,) * 8,
+        scratch_shapes=[pltpu.SemaphoreType.DMA((4,))],
         compiler_params=params,
         name="middle",
     )(
         recv,
-        exchanged,
         partial,
         left_vector,
-        bucket_fill,
-        recurrence,
         source_index,
         source_coeffs,
         source_vector,
         knot_vector,
         own,
+        *later,
+        knot_coeffs,
+        band_start,
+        *moved,
     )
     sums = lax.all_to_all(sums, ("src", "tm"), split_axis=0, concat_axis=0, tiled=True)
     like = [shape(x.shape, F32) for x in (left_vector, source_vector, knot_vector)]
     outs = pl.pallas_call(
         functools.partial(after_kernel, total_obs, unknowns),
-        out_shape=(like[0], like[1], like[2], like[1], like[2], like[1], like[2], shape((1, LANES), F32)),
-        in_specs=[VMEM, SMEM] + [VMEM] * 9,
-        out_specs=(VMEM,) * 8,
+        out_shape=(like[0], like[1], like[2], like[1], like[2], like[1], like[2], shape((4,), F32)),
+        in_specs=[VMEM] * 11,
+        out_specs=(VMEM,) * 7 + (SMEM,),
         compiler_params=params,
         name="after",
     )(
         sums,
-        recurrence,
+        own,
         raw,
         gradient_source,
         gradient_knot,
         source_vector,
         knot_vector,
-        source_search,
-        knot_search,
-        source_solution,
-        knot_solution,
-    )
-    return (*outs[:7], outs[7][0, :4])
+        *later,
+    )
+    return outs
 
 
 def solution(mesh):

time: 40.6 us -> 32.7 us (0.81)
  blocking collectives: 25.2 us -> 9.32 us
  waiting for transfers between devices: 1.74 us -> 8.57 us
  starting transfers between devices: 4.38 us -> 9.4 us
  local copies, waits for them, and re-layouts: 2.62 us -> 0.07 us
  Pallas kernels: 4.92 us -> 4.23 us
  other arithmetic: 0.63 us -> 0 us
    all_to_all x1 -> x0, blocking collectives: 15.8 us -> none  [shards(): lax.all_to_all(send, ('src', 'tm'), split_axis=0, concat_axis=0, tiled=True)]
    all_to_all x1, waiting for transfers between devices: 1.74 us -> 5.23 us  [shards(): lax.all_to_all(send, ('src', 'tm'), split_axis=0, concat_axis=0, tiled=True)]
    ppermute x0 -> x2, waiting for transfers between devices: none -> 3.35 us  [the longest x1 3.34 us: shards(): lax.ppermute(band_start, 'tm', shifted)]
    all_to_all x1, starting transfers between devices: 4.38 us -> 7.31 us  [shards(): lax.all_to_all(send, ('src', 'tm'), split_axis=0, concat_axis=0, tiled=True)]
    ppermute x0 -> x2, starting transfers between devices: none -> 2.09 us  [the longest x1 1.83 us: shards(): lax.ppermute(knot_coeffs, 'tm', shifted)]
    unnamed x28 -> x22, local copies, waits for them, and re-layouts: 2.1 us -> 0.07 us
    pallas_call x1, Pallas kernels: 2.04 us -> 1.24 us  [shards(): pl.pallas_call(functools.partial(middle_kernel, groups, slabs), out_shape...]
    transpose x1 -> x0, other arithmetic: 0.62 us -> none  [shards(): regroup = jnp.transpose(regroup, (1, 0, 2))]
  transfers between devices with their start and end apart: 1 -> 3, of which waited for: 1 -> 2; matrix products, arithmetic and copies ran while one was open for 0% -> 0% of each run, Pallas kernels for 4% -> 0%
where the time goes in v2:
time: 32.7 us; the launch traced here: 32.4 us
  starting transfers between devices  9.4 us (29%)
  blocking collectives  9.32 us (29%)
  waiting for transfers between devices  8.57 us (26%)
  Pallas kernels  4.23 us (13%)
  between operations  0.81 us (2%)
    all_to_all x1, blocking collectives, shards(): lax.all_to_all(sums, ('src', 'tm'), split_axis=0, concat_axis=0, tiled=True)  9.32 us
    all_to_all x1, starting transfers between devices, shards(): lax.all_to_all(send, ('src', 'tm'), split_axis=0, concat_axis=0, tiled=True)  7.31 us
    all_to_all x1, waiting for transfers between devices, shards(): lax.all_to_all(send, ('src', 'tm'), split_axis=0, concat_axis=0, tiled=True)  5.23 us
    ppermute x1, waiting for transfers between devices, shards(): lax.ppermute(band_start, 'tm', shifted)  3.34 us
    pallas_call x1, Pallas kernels, shards(): pl.pallas_call(functools.partial(before_kernel, groups, slabs), out_shape...  2.14 us
    ppermute x1, starting transfers between devices, shards(): lax.ppermute(knot_coeffs, 'tm', shifted)  1.83 us
    pallas_call x1, Pallas kernels, shards(): pl.pallas_call(functools.partial(middle_kernel, groups, slabs), out_shape...  1.24 us
    pallas_call x1, Pallas kernels, shards(): pl.pallas_call(functools.partial(after_kernel, total_obs, unknowns), out_...  0.85 us
  transfers between devices with their start and end apart: 3, of which 2 were waited for; matrix products, arithmetic and copies ran while one was open for 0% of the time, Pallas kernels for 0%

profile of v2, /device:TPU:0, one launch (start us, length us, event | category | flops | bytes accessed | tf_op | source)
XLA Modules:
  0.0 32.4 jit_solution(13144734196238848371)
XLA Ops:
  0.6 2.1 %before.1 = (f32[32,16,128]{2,1,0:T(8,128)}, f32[2,256]{1,0:T(2,128)S(1)}, f32[24,128]{1,0:T(8,128)S(1)}) custom-call(s32[2,256]{1,0:T(2,128)} %source_index.1, f32[5,2,256]{2,1,0:T(2,128)} %source_coeffs.1, f32[5,1024]{1,0:T(8,128)} %source_vector.3, f32[2,256]{1,0:T(2,128)} %left.1, s32[2]{0:T(128)} %bitcast.7, f32[3]{0:T(128)} %refs_5_.2, ...), custom_call_target="tpu_custom_call" | custom-call | tf_op jit(solution)/shard_map/before/pallas_call | solution.py:352
  2.8 0.0 copy-start.1
  2.8 0.0 copy-start.8
  2.8 0.0 copy-start
  2.8 0.0 copy-start.2
  2.8 0.0 copy-start.3
  2.8 0.0 copy-start.4
  2.9 0.0 copy-start.6
  2.9 0.0 copy-start.7
  2.9 0.0 copy-start.9
  2.9 0.0 copy-start.10
  2.9 7.3 %all-to-all-start = ((f32[32,16,128]{2,1,0:T(8,128)}), f32[32,16,128]{2,1,0:T(8,128)S(1)}, u32[]{:S(2)}, u32[]{:S(2)}) async-start(f32[32,16,128]{2,1,0:T(8,128)} %get-tuple-element.19), calls=%async_computation | async-start | bytes 524288 | tf_op jit(solution)/shard_map/all_to_all | solution.py:366
  10.2 0.0 copy-done.1
  10.2 0.0 copy-start.5
  10.2 1.8 %collective-permute-start = (f32[12,2,256]{2,1,0:T(2,128)S(1)}, f32[12,2,256]{2,1,0:T(2,128)S(1)}, u32[]{:S(2)}, u32[]{:S(2)}) collective-permute-start(f32[12,2,256]{2,1,0:T(2,128)S(1)} %copy-done.1), channel_id=1, source_target_pairs={{0,1},{1,0},{2,3},{3,2},{4,5},{5,4},{6,7},{7,6},{8,9},{9,8},{10,11... | collective-permute-start | bytes 73736 | tf_op jit(solution)/shard_map/ppermute | solution.py:338
  12.1 0.0 copy-done.8
  12.1 0.3 collective-permute-start.1
  12.3 3.3 %collective-permute-done.1.refs_7_ = s32[2,256]{1,0:T(2,128)S(1)} collective-permute-done((s32[2,256]{1,0:T(2,128)S(1)}, s32[2,256]{1,0:T(2,128)S(1)}, u32[]{:S(2)}, u32[]{:S(2)}) %collective-permute-start.1) | collective-permute-done | bytes 2080 | tf_op jit(solution)/shard_map/ppermute | solution.py:338
  15.7 0.0 collective-permute-done.refs_6_
  15.7 5.2 %all-to-all-done.recv = f32[32,16,128]{2,1,0:T(8,128)S(1)} async-done(((f32[32,16,128]{2,1,0:T(8,128)}), f32[32,16,128]{2,1,0:T(8,128)S(1)}, u32[]{:S(2)}, u32[]{:S(2)}) %all-to-all-start) | async-done | bytes 262176 | tf_op jit(solution)/shard_map/all_to_all | solution.py:366
  20.9 0.0 copy-done
  20.9 0.0 copy-done.2
  20.9 0.0 copy-done.3
  20.9 0.0 copy-done.4
  20.9 0.0 copy-done.6
  20.9 0.0 copy-done.7
  20.9 0.0 copy-done.9
  21.0 0.0 copy-done.10
  21.0 0.0 copy-done.5
  21.0 1.2 %middle.1 = (f32[2,256]{1,0:T(2,128)S(1)}, f32[5,1024]{1,0:T(8,128)S(1)}, f32[3,1,256]{2,1,0:T(1,128)S(1)}, f32[32,128]{1,0:T(8,128)S(1)}, f32[5,1024]{1,0:T(8,1...) custom-call(f32[32,16,128]{2,1,0:T(8,128)S(1)} %all-to-all-done.recv, ...), custom_call_target="tpu_custom_call" | custom-call | tf_op jit(solution)/shard_map/middle/pallas_call | solution.py:368
  22.2 9.3 %all_to_all.16 = f32[32,1,128]{2,1,0:T(1,128)S(1)} all-to-all(f32[32,1,128]{2,1,0:T(1,128)S(1)} %bitcast.6), channel_id=1, replica_groups=mesh['src'=16,'tm'=2] {'src','tm'}, dimensions={0} | all-to-all | bytes 32768 | tf_op jit(solution)/shard_map/all_to_all | solution.py:396
  31.6 0.8 %after.1 = (f32[2,256]{1,0:T(2,128)}, f32[5,1024]{1,0:T(8,128)}, f32[3,1,256]{2,1,0:T(1,128)}, f32[5,1024]{1,0:T(8,128)}, f32[3,1,256]{2,1,0:T(1,128)}, /*index=...) custom-call(f32[32,128]{1,0:T(8,128)S(1)} %bitcast.5, f32[24,128]{1,0:T(8,128)S(1)} %get-tuple-element.21.own, ...), custom_call_target="tpu_custom_call" | custom-call | tf_op jit(solution)/shard_map/after/pallas_call | solution.py:398
Async XLA Ops:
  2.8 7.4 %copy-start.1 = (f32[12,2,256]{2,1,0:T(2,128)S(1)}, f32[12,2,256]{2,1,0:T(2,128)}, u32[]{:S(2)}) copy-start(f32[12,2,256]{2,1,0:T(2,128)} %refs_4_.1) | copy-start | bytes 73732
  2.8 9.3 %copy-start.8 = (s32[2,256]{1,0:T(2,128)S(1)}, s32[2,256]{1,0:T(2,128)}, u32[]{:S(2)}) copy-start(s32[2,256]{1,0:T(2,128)} %refs_5_.3) | copy-start | bytes 6148
  2.8 18.1 %copy-start = (f32[5,1024]{1,0:T(8,128)S(1)}, f32[5,1024]{1,0:T(8,128)}, u32[]{:S(2)}) copy-start(f32[5,1024]{1,0:T(8,128)} %source_vector.3) | copy-start | bytes 61444
  2.8 18.1 %copy-start.2 = (f32[5,2,256]{2,1,0:T(2,128)S(1)}, f32[5,2,256]{2,1,0:T(2,128)}, u32[]{:S(2)}) copy-start(f32[5,2,256]{2,1,0:T(2,128)} %source_coeffs.1) | copy-start | bytes 30724
  2.8 18.1 %copy-start.3 = (f32[5,1024]{1,0:T(8,128)S(1)}, f32[5,1024]{1,0:T(8,128)}, u32[]{:S(2)}) copy-start(f32[5,1024]{1,0:T(8,128)} %refs_0_.3) | copy-start | bytes 61444
  2.8 18.1 %copy-start.4 = (f32[5,1024]{1,0:T(8,128)S(1)}, f32[5,1024]{1,0:T(8,128)}, u32[]{:S(2)}) copy-start(f32[5,1024]{1,0:T(8,128)} %refs_2_.3) | copy-start | bytes 61444
  2.9 18.1 %copy-start.6 = (s32[2,256]{1,0:T(2,128)S(1)}, s32[2,256]{1,0:T(2,128)}, u32[]{:S(2)}) copy-start(s32[2,256]{1,0:T(2,128)} %source_index.1) | copy-start | bytes 6148
  2.9 18.1 %copy-start.7 = (f32[2,256]{1,0:T(2,128)S(1)}, f32[2,256]{1,0:T(2,128)}, u32[]{:S(2)}) copy-start(f32[2,256]{1,0:T(2,128)} %left.1) | copy-start | bytes 6148
  2.9 18.1 %copy-start.9 = (f32[3,1,256]{2,1,0:T(1,128)S(1)}, f32[3,1,256]{2,1,0:T(1,128)}, u32[]{:S(2)}) copy-start(f32[3,1,256]{2,1,0:T(1,128)} %refs_1_.3) | copy-start | bytes 9220
  2.9 18.1 %copy-start.10 = (f32[3,1,256]{2,1,0:T(1,128)S(1)}, f32[3,1,256]{2,1,0:T(1,128)}, u32[]{:S(2)}) copy-start(f32[3,1,256]{2,1,0:T(1,128)} %refs_3_.3) | copy-start | bytes 9220
  2.9 18.0 %all-to-all-start = ((f32[32,16,128]{2,1,0:T(8,128)}), f32[32,16,128]{2,1,0:T(8,128)S(1)}, u32[]{:S(2)}, u32[]{:S(2)}) async-start(f32[32,16,128]{2,1,0:T(8,128)} %get-tuple-element.19), calls=%async_computation | async-start | bytes 524288 | tf_op jit(solution)/shard_map/all_to_all | solution.py:366
  10.2 10.7 %copy-start.5 = (f32[3,1,256]{2,1,0:T(1,128)S(1)}, f32[3,1,256]{2,1,0:T(1,128)}, u32[]{:S(2)}) copy-start(f32[3,1,256]{2,1,0:T(1,128)} %knots.3) | copy-start | bytes 9220
  10.2 5.4 %collective-permute-start = (f32[12,2,256]{2,1,0:T(2,128)S(1)}, f32[12,2,256]{2,1,0:T(2,128)S(1)}, u32[]{:S(2)}, u32[]{:S(2)}) collective-permute-start(f32[12,2,256]{2,1,0:T(2,128)S(1)} %copy-done.1), channel_id=1, source_target_pairs={{0,1},{1,0},{2,3},{3,2},{4,5},{5,4},{6,7},{7,6},{8,9},{9,8},{10,11... | collective-permute-start | bytes 73736 | tf_op jit(solution)/shard_map/ppermute | solution.py:338
  12.1 3.6 %collective-permute-start.1 = (s32[2,256]{1,0:T(2,128)S(1)}, s32[2,256]{1,0:T(2,128)S(1)}, u32[]{:S(2)}, u32[]{:S(2)}) collective-permute-start(s32[2,256]{1,0:T(2,128)S(1)} %copy-done.8), channel_id=1, source_target_pairs={{0,1},{1,0},{2,3},{3,2},{4,5},{5,4},{6,7},{7,6},{8,9},{9,8},{10,11... | collective-permute-start | bytes 6152 | tf_op jit(solution)/shard_map/ppermute | solution.py:338

commit v3 on v2

--- a/solution.py
+++ b/solution.py
@@ -9,6 +9,7 @@
 
 KB = 4
 ROWS = 3 * KB
+BLOCK = 14
 LANES = 128
 EPSILON = 1e-06
 F32 = jnp.float32
@@ -96,12 +97,15 @@
 
 
 def before_kernel(groups, slabs, *refs):
-    count = 9
-    sources, (send, partial_out, own) = refs[:count], refs[count : count + 3]
-    targets, semaphores = refs[count + 3 : -1], refs[-1]
-    for copy in fetch(sources, targets, semaphores):
+    sources, (send, partial_out, own), targets, semaphores = refs[:13], refs[13:16], refs[16:29], refs[29]
+    order = [*range(7), 11, 12, *range(7, 11)]
+    copies = fetch([sources[k] for k in order], [targets[k] for k in order], semaphores)
+    for copy in copies[:9]:
         copy.wait()
-    source_index, source_coeffs, source_vector, left, fill, recurrence, knot_coeffs, band, knots = targets
+    fill, recurrence, source_index, source_coeffs, source_vector, left, knot_coeffs, band, knots = (
+        *targets[-2:],
+        *targets[:7],
+    )
     buckets, capacity = left.shape
     source_dev = source_vector.shape[1]
     knot_dev = knots.shape[2]
@@ -119,6 +123,7 @@
         partial.append(jnp.where(slot < fill[t], image - alpha * left[pl.ds(t, 1), :], 0.0))
         partial_out[pl.ds(t, 1), :] = partial[t]
 
+    my_slab = lax.axis_index("tm")
     total = jnp.zeros((groups, 1), F32)
     before = jnp.where(iota((capacity, capacity), 0) < iota((capacity, capacity), 1), 1.0, 0.0).astype(BF16)
     targets, columns = [], []
@@ -133,9 +138,11 @@
         local = (bands_i - owner * bands).astype(F32)
         place = (slot + i * capacity).astype(F32)
         zero = jnp.zeros((1, capacity), F32)
-        coeffs = knot_coeffs[:, i, :]
+        here = my_slab == i
+        coeffs = jnp.where(here & (slot >= fill[i]), 0.0, knot_coeffs[:, i, :])
+        known = jnp.where(here, partial[i], 0.0)
         columns.append(
-            jnp.concatenate([coeffs[: ROWS // 2], local, zero, coeffs[ROWS // 2 :], place, zero], axis=0)
+            jnp.concatenate([coeffs[: ROWS // 2], local, known, coeffs[ROWS // 2 :], place, zero], axis=0)
         )
     packed = put(jnp.concatenate(columns, axis=1), jnp.concatenate(targets, axis=1), groups * bands)
 
@@ -154,9 +161,12 @@
     own[16:, :] = scalars
     knot_rows = halves(rows, low8)[: ROWS // 2]
 
-    last = iota((8, LANES), 0) == 7
-    first = [
-        jnp.concatenate([knot_rows] + [partial[t][:, k * LANES : (k + 1) * LANES] for k in range(2)], axis=0)
+    other = [
+        jnp.concatenate(
+            [partial[t][:, k * LANES : (k + 1) * LANES] for k in range(capacity // LANES)]
+            + [jnp.full((8 - capacity // LANES, LANES), fill[t].astype(F32))],
+            axis=0,
+        )
         for t in range(buckets)
     ]
     for g in range(groups // 2):
@@ -165,9 +175,11 @@
         pair = (jnp.where(low8, tile[:8], turned[8:]), jnp.where(low8, turned[:8], tile[8:]))
         for h in range(2):
             for t in range(slabs):
-                block = (2 * g + h) * slabs + t
-                send[block, 0:8, :] = first[t]
-                send[block, 8:16, :] = jnp.where(last, fill[t].astype(F32), pair[h])
+                row = ((2 * g + h) * slabs + t) * BLOCK
+                send[row : row + 8, :] = jnp.where(my_slab == t, pair[h], other[t])
+                send[row + 8 : row + BLOCK, :] = knot_rows
+    for copy in copies[9:]:
+        copy.wait()
 
 
 def joined(even, odd, low, bands):
@@ -177,7 +189,6 @@
 
 
 def middle_kernel(groups, slabs, recv, partial, left, source_index, source_coeffs, source_vector, knots, own, *refs):
-    later_in, refs, semaphores = refs[:4], refs[4:-1], refs[-1]
     buckets, capacity = left.shape
     source_dev = source_vector.shape[1]
     knot_dev = knots.shape[2]
@@ -188,28 +199,31 @@
     packets = groups * bands
     alpha = own[16:17, 0:1]
     my_slab = lax.axis_index("tm")
-    moved, (raw_out, gradient_source, gradient_knot, sums) = refs[: 2 * slabs], refs[2 * slabs : -4]
-    later = fetch(later_in, refs[-4:], semaphores)
+    moved, (raw_out, gradient_source, gradient_knot, sums) = refs[: 2 * slabs], refs[2 * slabs :]
     low = iota((8, LANES), 1) < bands
     slot = iota((1, capacity), 1).astype(F32)
 
     indices, weighted = [], []
     squares = jnp.zeros((1, capacity), F32)
     cross = jnp.zeros((1, capacity), F32)
-    for k in range(slabs):
-        t = lax.rem(my_slab + (slabs - k), slabs)
-        table = jnp.concatenate(
-            [
-                joined(recv[2 * g * slabs + t, 0:8, :], recv[(2 * g + 1) * slabs + t, 0:8, :], low, bands)
-                for g in range(groups // 2)
-            ],
-            axis=1,
-        )
-        block = moved[2 * k][:, my_slab, :]
-        coeffs = jnp.concatenate(
-            [pad_rows(block[: ROWS // 2], 8), pad_rows(block[ROWS // 2 :], 8)], axis=0
-        )
-        found = pick(table, moved[2 * k + 1][pl.ds(my_slab, 1), :])
+    def blocks(t, start):
+        rows = [((2 * g + h) * slabs + t) * BLOCK + start for g in range(groups // 2) for h in range(2)]
+        loaded = [recv[row : row + 8, :] for row in rows]
+        return jnp.concatenate([joined(*loaded[k : k + 2], low, bands) for k in range(0, groups, 2)], axis=1)
+
+    def of_slab(t, values):
+        result = values[0]
+        for k in range(1, slabs):
+            result = jnp.where(my_slab == (t + k) % slabs, values[k], result)
+        return result
+
+    coeffs_of = [moved[2 * k][:, my_slab, :] for k in range(slabs)]
+    bands_of = [moved[2 * k + 1][pl.ds(my_slab, 1), :] for k in range(slabs)]
+    gap = jnp.zeros((2, capacity), F32)
+    for t in range(slabs):
+        block = of_slab(t, coeffs_of)
+        coeffs = jnp.concatenate([gap, block[: ROWS // 2], gap, block[ROWS // 2 :]], axis=0)
+        found = pick(blocks(t, 6), of_slab(t, bands_of))
         image = jnp.sum(coeffs * found, axis=0, keepdims=True)
         raw = partial[pl.ds(t, 1), :] + jnp.where(slot < own[pl.ds(17 + t, 1), 0:1], image, 0.0)
         raw_out[pl.ds(t, 1), :] = raw
@@ -220,53 +234,59 @@
     gathered_sum = put(jnp.concatenate(weighted, axis=1), jnp.concatenate(indices, axis=1), source_dev)
     gradient_source[...] = gathered_sum[:5]
 
-    packet = jnp.concatenate(
-        [
-            joined(
-                recv[2 * g * slabs + my_slab, 8:16, :], recv[(2 * g + 1) * slabs + my_slab, 8:16, :], low, bands
-            )
-            for g in range(groups // 2)
-        ],
-        axis=1,
-    )
+    packet = blocks(0, 0)
+    for t in range(1, slabs):
+        packet = jnp.where(my_slab == t, blocks(t, 0), packet)
     band = packet[6:7].astype(I32)
     place = packet[14:15].astype(I32)
     inner = place & (capacity - 1)
-    sender = (iota((1, packets), 1) >> shift) * slabs + (place >> capacity_shift)
-    chosen = iota((devices, packets), 0) == sender
-    partials = jnp.concatenate([recv[:, 6, :], recv[:, 7, :]], axis=1)
-    found = pick(partials, inner)
-    fills = jnp.concatenate([recv[:, 15, :]] * (packets // LANES), axis=1)
-    partial_packet = jnp.sum(jnp.where(chosen, found, 0.0), axis=0, keepdims=True)
-    fill_packet = jnp.sum(jnp.where(chosen, fills, 0.0), axis=0, keepdims=True)
+    first = place >> capacity_shift
+    senders = WIDE // bands
+    member = senders * slabs
+    part = [recv[pl.ds(k, devices, stride=BLOCK), :] for k in range(capacity // LANES + 1)]
+    partials = jnp.concatenate(part[:-1], axis=1)
+    fills = jnp.concatenate([part[-1]] * (WIDE // LANES), axis=1)
+    row = iota((member, WIDE), 0)
+    sender = (iota((1, WIDE), 1) >> shift) * slabs
+    found = []
+    for q in range(packets // WIDE):
+        lanes = slice(q * WIDE, (q + 1) * WIDE)
+        rows = slice(q * member, (q + 1) * member)
+        chosen = row == sender + first[:, lanes]
+        values = pick(partials[rows], inner[:, lanes])
+        valid = jnp.sum(jnp.where(chosen, fills[rows], 0.0), axis=0, keepdims=True)
+        found.append((jnp.sum(jnp.where(chosen, values, 0.0), axis=0, keepdims=True), valid))
+    partial_packet, fill_packet = (jnp.concatenate(x, axis=1) for x in zip(*found))
     image = jnp.sum(packet * pick(own[0:16, 0:bands], band), axis=0, keepdims=True)
-    raw = jnp.where(inner.astype(F32) < fill_packet, partial_packet + image, 0.0)
-    collected = put(packet * raw, band, bands)
-    hit = iota((bands, knot_dev), 0) == (iota((bands, knot_dev), 1) >> 2)
-    spread = fold3(dot(split3(collected), jnp.where(hit, 1.0, 0.0).astype(BF16)))
+    known = first == my_slab
+    partial_packet = jnp.where(known, packet[7:8], partial_packet)
+    raw = jnp.where(known | (inner.astype(F32) < fill_packet), partial_packet + image, 0.0)
+    hit = (iota((knot_dev, packets), 0) >> 2) == band
+    spread = fold3(dot_nt(split3(packet * raw), jnp.where(hit, 1.0, 0.0).astype(BF16)))
     held, axis_of, offset = row_parts((16, knot_dev))
     spread = jnp.where(held & ((iota((16, knot_dev), 1) & (KB - 1)) == offset), spread, 0.0)
-    knot_squares = jnp.zeros((1, knot_dev), F32)
-    knot_old = jnp.zeros((1, knot_dev), F32)
     for a in range(3):
-        total = jnp.sum(jnp.where(axis_of == a, spread, 0.0), axis=0, keepdims=True)
-        gradient_knot[a] = total
-        knot_squares = knot_squares + total * total
-        knot_old = knot_old + knots[a] * knots[a]
-
-    own_squares = jnp.sum(squares)
-    cross_sum = jnp.sum(cross)
-    gradient_squares = jnp.sum(gathered_sum * gathered_sum) + jnp.sum(knot_squares)
+        gradient_knot[a] = jnp.sum(jnp.where(axis_of == a, spread, 0.0), axis=0, keepdims=True)
+
+    def across(x):
+        x = jnp.sum(x, axis=0, keepdims=True)
+        return functools.reduce(jnp.add, [x[:, k : k + LANES] for k in range(0, x.shape[1], LANES)])
+
     old = source_vector[...]
-    old_squares = jnp.sum(old * old) + jnp.sum(knot_old)
-    lane = iota((devices, LANES), 1)
-    sums[...] = jnp.where(
-        lane == 0,
-        own_squares,
-        jnp.where(lane == 1, gradient_squares, jnp.where(lane == 2, cross_sum, old_squares)),
-    )
-    for copy in later:
-        copy.wait()
+    old_knots = sum(knots[a] * knots[a] for a in range(3))
+    new_knots = sum(gradient_knot[a] * gradient_knot[a] for a in range(3))
+    parts = (
+        across(squares),
+        across(gathered_sum * gathered_sum) + across(new_knots),
+        across(cross),
+        across(old * old) + across(old_knots),
+    )
+    quarter = iota((8, LANES), 0)
+    stacked = jnp.zeros((8, LANES), F32)
+    for k, part in enumerate(parts):
+        stacked = jnp.where(quarter == k, part, stacked)
+    totals = jnp.where(quarter == iota((8, LANES), 1), jnp.sum(stacked, axis=1, keepdims=True), 0.0)
+    sums[...] = jnp.broadcast_to(jnp.sum(totals, axis=0, keepdims=True), sums.shape)
 
 
 def after_kernel(total_obs, unknowns, sums, own, raw, gradient_source, gradient_knot, source_vector, knots, source_search, knot_search, source_solution, knot_solution, left_next, source_next, knot_next, search_source, search_knot, solution_source, solution_knot, recurrence_next):
@@ -332,63 +352,67 @@
     params = pltpu.CompilerParams(vmem_limit_bytes=48 * 1024 * 1024)
     shape = jax.ShapeDtypeStruct
 
-    moved = []
-    for k in range(1, slabs):
-        shifted = [(t, (t + k) % slabs) for t in range(slabs)]
-        moved += [lax.ppermute(knot_coeffs, "tm", shifted), lax.ppermute(band_start, "tm", shifted)]
-
     fill = bucket_fill.reshape(-1)
     operands = (
         source_index,
         source_coeffs,
         source_vector,
         left_vector,
-        fill,
-        recurrence,
         knot_coeffs,
         band_start,
         knot_vector,
-    )
-    send, partial, own = pl.pallas_call(
+        source_search,
+        knot_search,
+        source_solution,
+        knot_solution,
+        fill,
+        recurrence,
+    )
+    send, partial, own, *held = pl.pallas_call(
         functools.partial(before_kernel, groups, slabs),
         out_shape=(
-            pltpu.VMEM((devices, 16, LANES), F32),
+            shape((devices * BLOCK, LANES), F32),
             shape((buckets, capacity), F32),
             shape((16 + 8 * pl.cdiv(1 + buckets, 8), LANES), F32),
+            *(pltpu.VMEM(x.shape, x.dtype) for x in operands[:-2]),
         ),
         in_specs=[HBM] * len(operands),
-        out_specs=(VMEM, VMEM, VMEM),
-        scratch_shapes=[(pltpu.SMEM if x.ndim == 1 else pltpu.VMEM)(x.shape, x.dtype) for x in operands]
+        out_specs=(VMEM,) * 14,
+        scratch_shapes=[pltpu.SMEM(x.shape, x.dtype) for x in operands[-2:]]
         + [pltpu.SemaphoreType.DMA((len(operands),))],
         compiler_params=params,
         name="before",
     )(*(pltpu.with_memory_space_constraint(x, pltpu.HBM) for x in operands))
+    source_index, source_coeffs, source_vector, left_held, knot_coeffs, band_start, knots_held, *later = held
+    moved = []
+    for k in range(1, slabs):
+        shifted = [(t, (t + k) % slabs) for t in range(slabs)]
+        moved += [lax.ppermute(knot_coeffs, "tm", shifted), lax.ppermute(band_start, "tm", shifted)]
+
+    send = send.reshape(devices * BLOCK, 1, LANES)
     recv = lax.all_to_all(send, ("src", "tm"), split_axis=0, concat_axis=0, tiled=True)
-    later = (source_search, knot_search, source_solution, knot_solution)
-    raw, gradient_source, gradient_knot, sums, *later = pl.pallas_call(
+    recv = recv.reshape(devices * BLOCK, LANES)
+    raw, gradient_source, gradient_knot, sums = pl.pallas_call(
         functools.partial(middle_kernel, groups, slabs),
         out_shape=(
             shape((buckets, capacity), F32),
             shape((5, source_dev), F32),
             shape((3, 1, knot_dev), F32),
             shape((devices, LANES), F32),
-            *(shape(x.shape, F32) for x in later),
         ),
-        in_specs=[VMEM] * 8 + [HBM] * 4 + [VMEM] * (2 * slabs),
-        out_specs=(VMEM,) * 8,
-        scratch_shapes=[pltpu.SemaphoreType.DMA((4,))],
+        in_specs=[VMEM] * (8 + 2 * slabs),
+        out_specs=(VMEM,) * 4,
         compiler_params=params,
         name="middle",
     )(
         recv,
         partial,
-        left_vector,
+        left_held,
         source_index,
         source_coeffs,
         source_vector,
-        knot_vector,
+        knots_held,
         own,
-        *later,
         knot_coeffs,
         band_start,
         *moved,
@@ -409,7 +433,7 @@
         gradient_source,
         gradient_knot,
         source_vector,
-        knot_vector,
+        knots_held,
         *later,
     )
     return outs

time: 32.7 us -> 31.6 us (0.966)
  waiting for transfers between devices: 8.57 us -> 8.08 us
    all_to_all x1, waiting for transfers between devices: 5.23 us -> 4.72 us  [shards(): lax.all_to_all(send, ('src', 'tm'), split_axis=0, concat_axis=0, tiled=True)]
where the time goes in v3:
time: 31.6 us; the launch traced here: 31.3 us
  starting transfers between devices  9.4 us (30%)
  blocking collectives  9.13 us (29%)
  waiting for transfers between devices  8.08 us (26%)
  Pallas kernels  4.02 us (13%)
  between operations  0.66 us (2%)
    all_to_all x1, blocking collectives, shards(): lax.all_to_all(sums, ('src', 'tm'), split_axis=0, concat_axis=0, tiled=True)  9.13 us
    all_to_all x1, starting transfers between devices, shards(): lax.all_to_all(send, ('src', 'tm'), split_axis=0, concat_axis=0, tiled=True)  7.3 us
    all_to_all x1, waiting for transfers between devices, shards(): lax.all_to_all(send, ('src', 'tm'), split_axis=0, concat_axis=0, tiled=True)  4.72 us
    ppermute x1, waiting for transfers between devices, shards(): lax.ppermute(band_start, 'tm', shifted)  3.36 us
    pallas_call x1, Pallas kernels, shards(): pl.pallas_call(functools.partial(before_kernel, groups, slabs), out_shape...  2.19 us
    ppermute x1, starting transfers between devices, shards(): lax.ppermute(knot_coeffs, 'tm', shifted)  1.83 us
    pallas_call x1, Pallas kernels, shards(): pl.pallas_call(functools.partial(middle_kernel, groups, slabs), out_shape...  0.98 us
    pallas_call x1, Pallas kernels, shards(): pl.pallas_call(functools.partial(after_kernel, total_obs, unknowns), out_...  0.85 us
  transfers between devices with their start and end apart: 3, of which 2 were waited for; matrix products, arithmetic and copies ran while one was open for 0% of the time, Pallas kernels for 0%

profile of v3, /device:TPU:0, one launch (start us, length us, event | category | flops | bytes accessed | tf_op | source)
XLA Modules:
  0.0 31.3 jit_solution(3844801119303750134)
XLA Ops:
  0.6 2.2 %before.1 = (f32[448,128]{1,0:T(8,128)}, f32[2,256]{1,0:T(2,128)S(1)}, f32[24,128]{1,0:T(8,128)S(1)}, s32[2,256]{1,0:T(2,128)S(1)}, f32[5,2,256]{2,1,0:T(2,128)S...) custom-call(s32[2,256]{1,0:T(2,128)} %refs_0_.1, ...), custom_call_target="tpu_custom_call" | custom-call | tf_op jit(solution)/shard_map/before/pallas_call | solution.py:371
  2.8 7.3 %all-to-all-start = ((f32[448,1,128]{2,1,0:T(1,128)}), f32[448,1,128]{2,1,0:T(1,128)S(1)}, u32[]{:S(2)}, u32[]{:S(2)}) async-start(f32[448,1,128]{2,1,0:T(1,128)} %bitcast.2), calls=%async_computation | async-start | bytes 458752 | tf_op jit(solution)/shard_map/all_to_all | solution.py:393
  10.1 1.8 %collective-permute-start = (f32[12,2,256]{2,1,0:T(2,128)S(1)}, f32[12,2,256]{2,1,0:T(2,128)S(1)}, u32[]{:S(2)}, u32[]{:S(2)}) collective-permute-start(f32[12,2,256]{2,1,0:T(2,128)S(1)} %get-tuple-element.34.refs_0_), channel_id=1, source_target_pairs={{0,1},{1,0},{2,3},{3,2},{4,5},{5,4},{6,7},{7,6},{8,9},{9,8},{10,11... | collective-permute-start | bytes 73736 | tf_op jit(solution)/shard_map/ppermute | solution.py:390
  12.0 0.3 collective-permute-start.1
  12.2 3.4 %collective-permute-done.1.refs_3_ = s32[2,256]{1,0:T(2,128)S(1)} collective-permute-done((s32[2,256]{1,0:T(2,128)S(1)}, s32[2,256]{1,0:T(2,128)S(1)}, u32[]{:S(2)}, u32[]{:S(2)}) %collective-permute-start.1) | collective-permute-done | bytes 2080 | tf_op jit(solution)/shard_map/ppermute | solution.py:390
  15.6 0.0 collective-permute-done.refs_2_
  15.6 4.7 %all-to-all-done = f32[448,1,128]{2,1,0:T(1,128)S(1)} async-done(((f32[448,1,128]{2,1,0:T(1,128)}), f32[448,1,128]{2,1,0:T(1,128)S(1)}, u32[]{:S(2)}, u32[]{:S(2)}) %all-to-all-start) | async-done | bytes 229408 | tf_op jit(solution)/shard_map/all_to_all | solution.py:393
  20.3 1.0 %middle.1 = (f32[2,256]{1,0:T(2,128)S(1)}, f32[5,1024]{1,0:T(8,128)S(1)}, f32[3,1,256]{2,1,0:T(1,128)S(1)}, f32[32,128]{1,0:T(8,128)S(1)}) custom-call(f32[448,128]{1,0:T(8,128)S(1)} %bitcast.9, f32[2,256]{1,0:T(2,128)S(1)} %get-tuple-element.27.partial, f32[2,256]{1,0:T(2,128)S(1)} %get-tuple-element.28.left, s32[2,256]{1,0:T(2,128)S(1)} %get-tuple-element.29.source_index, ...), custom_call_target="tpu_custom_call" | custom-call | tf_op jit(solution)/shard_map/middle/pallas_call | solution.py:395
  21.3 9.1 %all_to_all.16 = f32[32,1,128]{2,1,0:T(1,128)S(1)} all-to-all(f32[32,1,128]{2,1,0:T(1,128)S(1)} %bitcast.11), channel_id=1, replica_groups=mesh['src'=16,'tm'=2] {'src','tm'}, dimensions={0} | all-to-all | bytes 32768 | tf_op jit(solution)/shard_map/all_to_all | solution.py:420
  30.4 0.8 %after.1 = (f32[2,256]{1,0:T(2,128)}, f32[5,1024]{1,0:T(8,128)}, f32[3,1,256]{2,1,0:T(1,128)}, f32[5,1024]{1,0:T(8,128)}, f32[3,1,256]{2,1,0:T(1,128)}, /*index=...) custom-call(f32[32,128]{1,0:T(8,128)S(1)} %bitcast.10, f32[24,128]{1,0:T(8,128)S(1)} %get-tuple-element.33.own, ...), custom_call_target="tpu_custom_call" | custom-call | tf_op jit(solution)/shard_map/after/pallas_call | solution.py:422
Async XLA Ops:
  2.8 17.5 %all-to-all-start = ((f32[448,1,128]{2,1,0:T(1,128)}), f32[448,1,128]{2,1,0:T(1,128)S(1)}, u32[]{:S(2)}, u32[]{:S(2)}) async-start(f32[448,1,128]{2,1,0:T(1,128)} %bitcast.2), calls=%async_computation | async-start | bytes 458752 | tf_op jit(solution)/shard_map/all_to_all | solution.py:393
  10.1 5.5 %collective-permute-start = (f32[12,2,256]{2,1,0:T(2,128)S(1)}, f32[12,2,256]{2,1,0:T(2,128)S(1)}, u32[]{:S(2)}, u32[]{:S(2)}) collective-permute-start(f32[12,2,256]{2,1,0:T(2,128)S(1)} %get-tuple-element.34.refs_0_), channel_id=1, source_target_pairs={{0,1},{1,0},{2,3},{3,2},{4,5},{5,4},{6,7},{7,6},{8,9},{9,8},{10,11... | collective-permute-start | bytes 73736 | tf_op jit(solution)/shard_map/ppermute | solution.py:390
  12.0 3.6 %collective-permute-start.1 = (s32[2,256]{1,0:T(2,128)S(1)}, s32[2,256]{1,0:T(2,128)S(1)}, u32[]{:S(2)}, u32[]{:S(2)}) collective-permute-start(s32[2,256]{1,0:T(2,128)S(1)} %get-tuple-element.35.refs_1_), channel_id=1, source_target_pairs={{0,1},{1,0},{2,3},{3,2},{4,5},{5,4},{6,7},{7,6},{8,9},{9,8},{10,11... | collective-permute-start | bytes 6152 | tf_op jit(solution)/shard_map/ppermute | solution.py:390

commit v4 on v3

--- a/solution.py
+++ b/solution.py
@@ -21,11 +21,15 @@
     return lax.broadcasted_iota(I32, shape, axis)
 
 
-def split3(x):
+def thirds(x):
     hi = x.astype(BF16).astype(F32)
     rest = x - hi
     mid = rest.astype(BF16).astype(F32)
-    return jnp.concatenate([hi, mid, rest - mid], axis=0).astype(BF16)
+    return jnp.concatenate([hi, mid, rest - mid], axis=0)
+
+
+def split3(x):
+    return thirds(x).astype(BF16)
 
 
 def fold3(y):
@@ -58,14 +62,15 @@
 
 
 def put(values, index, count):
-    rows = values.shape[0]
+    rows = 3 * values.shape[0]
     width = min(count, WIDE)
     parts = count // width
     high = index >> (width.bit_length() - 1)
+    values = thirds(values)
     if parts > 1:
         values = jnp.concatenate([jnp.where(high == h, values, 0.0) for h in range(parts)], axis=0)
-    sums = fold3(dot_nt(split3(values), onehot(width, index & (width - 1))))
-    return jnp.concatenate([sums[h * rows : (h + 1) * rows] for h in range(parts)], axis=1)
+    sums = dot_nt(values.astype(BF16), onehot(width, index & (width - 1)))
+    return jnp.concatenate([fold3(sums[h * rows : (h + 1) * rows]) for h in range(parts)], axis=1)
 
 
 def onehot(count, index):
@@ -114,14 +119,6 @@
     alpha = recurrence[0]
     low8 = iota((8, LANES), 1) < bands
     slot = iota((1, capacity), 1)
-
-    index = jnp.concatenate([source_index[pl.ds(t, 1), :] for t in range(buckets)], axis=1)
-    picked = pick(pad_rows(source_vector[...], 8), index)[:5]
-    partial = []
-    for t in range(buckets):
-        image = jnp.sum(source_coeffs[:, t, :] * picked[:, t * capacity : (t + 1) * capacity], axis=0, keepdims=True)
-        partial.append(jnp.where(slot < fill[t], image - alpha * left[pl.ds(t, 1), :], 0.0))
-        partial_out[pl.ds(t, 1), :] = partial[t]
 
     my_slab = lax.axis_index("tm")
     total = jnp.zeros((groups, 1), F32)
@@ -135,9 +132,18 @@
         rank = jnp.sum(named * count, axis=0, keepdims=True).astype(I32)
         total = total + jnp.sum(named, axis=1, keepdims=True)
         targets.append(owner * bands + rank)
-        local = (bands_i - owner * bands).astype(F32)
+    index = jnp.concatenate([source_index[pl.ds(t, 1), :] for t in range(buckets)], axis=1)
+    picked = pick(pad_rows(source_vector[...], 8), index)[:5]
+    partial = []
+    for t in range(buckets):
+        image = jnp.sum(source_coeffs[:, t, :] * picked[:, t * capacity : (t + 1) * capacity], axis=0, keepdims=True)
+        partial.append(jnp.where(slot < fill[t], image - alpha * left[pl.ds(t, 1), :], 0.0))
+        partial_out[pl.ds(t, 1), :] = partial[t]
+
+    zero = jnp.zeros((1, capacity), F32)
+    for i in range(buckets):
+        local = (band[pl.ds(i, 1), :] & (bands - 1)).astype(F32)
         place = (slot + i * capacity).astype(F32)
-        zero = jnp.zeros((1, capacity), F32)
         here = my_slab == i
         coeffs = jnp.where(here & (slot >= fill[i]), 0.0, knot_coeffs[:, i, :])
         known = jnp.where(here, partial[i], 0.0)
@@ -203,9 +209,6 @@
     low = iota((8, LANES), 1) < bands
     slot = iota((1, capacity), 1).astype(F32)
 
-    indices, weighted = [], []
-    squares = jnp.zeros((1, capacity), F32)
-    cross = jnp.zeros((1, capacity), F32)
     def blocks(t, start):
         rows = [((2 * g + h) * slabs + t) * BLOCK + start for g in range(groups // 2) for h in range(2)]
         loaded = [recv[row : row + 8, :] for row in rows]
@@ -217,6 +220,10 @@
             result = jnp.where(my_slab == (t + k) % slabs, values[k], result)
         return result
 
+
+    indices, weighted = [], []
+    squares = jnp.zeros((1, capacity), F32)
+    cross = jnp.zeros((1, capacity), F32)
     coeffs_of = [moved[2 * k][:, my_slab, :] for k in range(slabs)]
     bands_of = [moved[2 * k + 1][pl.ds(my_slab, 1), :] for k in range(slabs)]
     gap = jnp.zeros((2, capacity), F32)
@@ -231,9 +238,6 @@
         cross = cross + raw * (raw + alpha * left[pl.ds(t, 1), :])
         indices.append(source_index[pl.ds(t, 1), :])
         weighted.append(pad_rows(source_coeffs[:, t, :] * raw, 8))
-    gathered_sum = put(jnp.concatenate(weighted, axis=1), jnp.concatenate(indices, axis=1), source_dev)
-    gradient_source[...] = gathered_sum[:5]
-
     packet = blocks(0, 0)
     for t in range(1, slabs):
         packet = jnp.where(my_slab == t, blocks(t, 0), packet)
@@ -260,14 +264,16 @@
     image = jnp.sum(packet * pick(own[0:16, 0:bands], band), axis=0, keepdims=True)
     known = first == my_slab
     partial_packet = jnp.where(known, packet[7:8], partial_packet)
-    raw = jnp.where(known | (inner.astype(F32) < fill_packet), partial_packet + image, 0.0)
+    packet_raw = jnp.where(known | (inner.astype(F32) < fill_packet), partial_packet + image, 0.0)
     hit = (iota((knot_dev, packets), 0) >> 2) == band
-    spread = fold3(dot_nt(split3(packet * raw), jnp.where(hit, 1.0, 0.0).astype(BF16)))
+    spread = fold3(dot_nt(split3(packet * packet_raw), jnp.where(hit, 1.0, 0.0).astype(BF16)))
     held, axis_of, offset = row_parts((16, knot_dev))
     spread = jnp.where(held & ((iota((16, knot_dev), 1) & (KB - 1)) == offset), spread, 0.0)
     for a in range(3):
         gradient_knot[a] = jnp.sum(jnp.where(axis_of == a, spread, 0.0), axis=0, keepdims=True)
 
+    gathered_sum = put(jnp.concatenate(weighted, axis=1), jnp.concatenate(indices, axis=1), source_dev)
+    gradient_source[...] = gathered_sum[:5]
     def across(x):
         x = jnp.sum(x, axis=0, keepdims=True)
         return functools.reduce(jnp.add, [x[:, k : k + LANES] for k in range(0, x.shape[1], LANES)])

time: 31.6 us -> 31.3 us (level)
  no operation moved by 1% of the time
where the time goes in v4:
time: 31.3 us; the launch traced here: 31.1 us
  starting transfers between devices  9.39 us (30%)
  blocking collectives  9.13 us (29%)
  waiting for transfers between devices  8.08 us (26%)
  Pallas kernels  3.79 us (12%)
  between operations  0.66 us (2%)
    all_to_all x1, blocking collectives, shards(): lax.all_to_all(sums, ('src', 'tm'), split_axis=0, concat_axis=0, tiled=True)  9.13 us
    all_to_all x1, starting transfers between devices, shards(): lax.all_to_all(send, ('src', 'tm'), split_axis=0, concat_axis=0, tiled=True)  7.3 us
    all_to_all x1, waiting for transfers between devices, shards(): lax.all_to_all(send, ('src', 'tm'), split_axis=0, concat_axis=0, tiled=True)  4.72 us
    ppermute x1, waiting for transfers between devices, shards(): lax.ppermute(band_start, 'tm', shifted)  3.36 us
    pallas_call x1, Pallas kernels, shards(): pl.pallas_call(functools.partial(before_kernel, groups, slabs), out_shape...  2.18 us
    ppermute x1, starting transfers between devices, shards(): lax.ppermute(knot_coeffs, 'tm', shifted)  1.83 us
    pallas_call x1, Pallas kernels, shards(): pl.pallas_call(functools.partial(after_kernel, total_obs, unknowns), out_...  0.85 us
    pallas_call x1, Pallas kernels, shards(): pl.pallas_call(functools.partial(middle_kernel, groups, slabs), out_shape...  0.77 us
  transfers between devices with their start and end apart: 3, of which 2 were waited for; matrix products, arithmetic and copies ran while one was open for 0% of the time, Pallas kernels for 0%

profile of v4, /device:TPU:0, one launch (start us, length us, event | category | flops | bytes accessed | tf_op | source)
XLA Modules:
  0.0 31.1 jit_solution(15174144962386502953)
XLA Ops:
  0.6 2.2 %before.1 = (f32[448,128]{1,0:T(8,128)}, f32[2,256]{1,0:T(2,128)S(1)}, f32[24,128]{1,0:T(8,128)S(1)}, s32[2,256]{1,0:T(2,128)S(1)}, f32[5,2,256]{2,1,0:T(2,128)S...) custom-call(s32[2,256]{1,0:T(2,128)} %refs_0_.1, ...), custom_call_target="tpu_custom_call" | custom-call | tf_op jit(solution)/shard_map/before/pallas_call | solution.py:377
  2.8 7.3 %all-to-all-start = ((f32[448,1,128]{2,1,0:T(1,128)}), f32[448,1,128]{2,1,0:T(1,128)S(1)}, u32[]{:S(2)}, u32[]{:S(2)}) async-start(f32[448,1,128]{2,1,0:T(1,128)} %bitcast.2), calls=%async_computation | async-start | bytes 458752 | tf_op jit(solution)/shard_map/all_to_all | solution.py:399
  10.1 1.8 %collective-permute-start = (f32[12,2,256]{2,1,0:T(2,128)S(1)}, f32[12,2,256]{2,1,0:T(2,128)S(1)}, u32[]{:S(2)}, u32[]{:S(2)}) collective-permute-start(f32[12,2,256]{2,1,0:T(2,128)S(1)} %get-tuple-element.34.refs_0_), channel_id=1, source_target_pairs={{0,1},{1,0},{2,3},{3,2},{4,5},{5,4},{6,7},{7,6},{8,9},{9,8},{10,11... | collective-permute-start | bytes 73736 | tf_op jit(solution)/shard_map/ppermute | solution.py:396
  12.0 0.3 collective-permute-start.1
  12.2 3.4 %collective-permute-done.1.refs_3_ = s32[2,256]{1,0:T(2,128)S(1)} collective-permute-done((s32[2,256]{1,0:T(2,128)S(1)}, s32[2,256]{1,0:T(2,128)S(1)}, u32[]{:S(2)}, u32[]{:S(2)}) %collective-permute-start.1) | collective-permute-done | bytes 2080 | tf_op jit(solution)/shard_map/ppermute | solution.py:396
  15.6 0.0 collective-permute-done.refs_2_
  15.6 4.7 %all-to-all-done = f32[448,1,128]{2,1,0:T(1,128)S(1)} async-done(((f32[448,1,128]{2,1,0:T(1,128)}), f32[448,1,128]{2,1,0:T(1,128)S(1)}, u32[]{:S(2)}, u32[]{:S(2)}) %all-to-all-start) | async-done | bytes 229408 | tf_op jit(solution)/shard_map/all_to_all | solution.py:399
  20.3 0.8 %middle.1 = (f32[2,256]{1,0:T(2,128)S(1)}, f32[5,1024]{1,0:T(8,128)S(1)}, f32[3,1,256]{2,1,0:T(1,128)S(1)}, f32[32,128]{1,0:T(8,128)S(1)}) custom-call(f32[448,128]{1,0:T(8,128)S(1)} %bitcast.9, f32[2,256]{1,0:T(2,128)S(1)} %get-tuple-element.27.partial, f32[2,256]{1,0:T(2,128)S(1)} %get-tuple-element.28.left, s32[2,256]{1,0:T(2,128)S(1)} %get-tuple-element.29.source_index, ...), custom_call_target="tpu_custom_call" | custom-call | tf_op jit(solution)/shard_map/middle/pallas_call | solution.py:401
  21.1 9.1 %all_to_all.16 = f32[32,1,128]{2,1,0:T(1,128)S(1)} all-to-all(f32[32,1,128]{2,1,0:T(1,128)S(1)} %bitcast.11), channel_id=1, replica_groups=mesh['src'=16,'tm'=2] {'src','tm'}, dimensions={0} | all-to-all | bytes 32768 | tf_op jit(solution)/shard_map/all_to_all | solution.py:426
  30.2 0.8 %after.1 = (f32[2,256]{1,0:T(2,128)}, f32[5,1024]{1,0:T(8,128)}, f32[3,1,256]{2,1,0:T(1,128)}, f32[5,1024]{1,0:T(8,128)}, f32[3,1,256]{2,1,0:T(1,128)}, /*index=...) custom-call(f32[32,128]{1,0:T(8,128)S(1)} %bitcast.10, f32[24,128]{1,0:T(8,128)S(1)} %get-tuple-element.33.own, ...), custom_call_target="tpu_custom_call" | custom-call | tf_op jit(solution)/shard_map/after/pallas_call | solution.py:428
Async XLA Ops:
  2.8 17.5 %all-to-all-start = ((f32[448,1,128]{2,1,0:T(1,128)}), f32[448,1,128]{2,1,0:T(1,128)S(1)}, u32[]{:S(2)}, u32[]{:S(2)}) async-start(f32[448,1,128]{2,1,0:T(1,128)} %bitcast.2), calls=%async_computation | async-start | bytes 458752 | tf_op jit(solution)/shard_map/all_to_all | solution.py:399
  10.1 5.5 %collective-permute-start = (f32[12,2,256]{2,1,0:T(2,128)S(1)}, f32[12,2,256]{2,1,0:T(2,128)S(1)}, u32[]{:S(2)}, u32[]{:S(2)}) collective-permute-start(f32[12,2,256]{2,1,0:T(2,128)S(1)} %get-tuple-element.34.refs_0_), channel_id=1, source_target_pairs={{0,1},{1,0},{2,3},{3,2},{4,5},{5,4},{6,7},{7,6},{8,9},{9,8},{10,11... | collective-permute-start | bytes 73736 | tf_op jit(solution)/shard_map/ppermute | solution.py:396
  12.0 3.6 %collective-permute-start.1 = (s32[2,256]{1,0:T(2,128)S(1)}, s32[2,256]{1,0:T(2,128)S(1)}, u32[]{:S(2)}, u32[]{:S(2)}) collective-permute-start(s32[2,256]{1,0:T(2,128)S(1)} %get-tuple-element.35.refs_1_), channel_id=1, source_target_pairs={{0,1},{1,0},{2,3},{3,2},{4,5},{5,4},{6,7},{7,6},{8,9},{9,8},{10,11... | collective-permute-start | bytes 6152 | tf_op jit(solution)/shard_map/ppermute | solution.py:396

commit v5 on v4

--- a/solution.py
+++ b/solution.py
@@ -181,7 +181,7 @@
         pair = (jnp.where(low8, tile[:8], turned[8:]), jnp.where(low8, turned[:8], tile[8:]))
         for h in range(2):
             for t in range(slabs):
-                row = ((2 * g + h) * slabs + t) * BLOCK
+                row = (t * groups + 2 * g + h) * BLOCK
                 send[row : row + 8, :] = jnp.where(my_slab == t, pair[h], other[t])
                 send[row + 8 : row + BLOCK, :] = knot_rows
     for copy in copies[9:]:
@@ -210,7 +210,7 @@
     slot = iota((1, capacity), 1).astype(F32)
 
     def blocks(t, start):
-        rows = [((2 * g + h) * slabs + t) * BLOCK + start for g in range(groups // 2) for h in range(2)]
+        rows = [(t * groups + s) * BLOCK + start for s in range(groups)]
         loaded = [recv[row : row + 8, :] for row in rows]
         return jnp.concatenate([joined(*loaded[k : k + 2], low, bands) for k in range(0, groups, 2)], axis=1)
 
@@ -247,18 +247,22 @@
     first = place >> capacity_shift
     senders = WIDE // bands
     member = senders * slabs
-    part = [recv[pl.ds(k, devices, stride=BLOCK), :] for k in range(capacity // LANES + 1)]
-    partials = jnp.concatenate(part[:-1], axis=1)
-    fills = jnp.concatenate([part[-1]] * (WIDE // LANES), axis=1)
     row = iota((member, WIDE), 0)
-    sender = (iota((1, WIDE), 1) >> shift) * slabs
+    sender = iota((1, WIDE), 1) >> shift
     found = []
     for q in range(packets // WIDE):
         lanes = slice(q * WIDE, (q + 1) * WIDE)
-        rows = slice(q * member, (q + 1) * member)
-        chosen = row == sender + first[:, lanes]
-        values = pick(partials[rows], inner[:, lanes])
-        valid = jnp.sum(jnp.where(chosen, fills[rows], 0.0), axis=0, keepdims=True)
+        part = [
+            jnp.concatenate(
+                [recv[pl.ds((i * groups + q * senders) * BLOCK + k, senders, stride=BLOCK), :] for i in range(slabs)],
+                axis=0,
+            )
+            for k in range(capacity // LANES + 1)
+        ]
+        chosen = row == first[:, lanes] * senders + sender
+        values = pick(jnp.concatenate(part[:-1], axis=1), inner[:, lanes])
+        fills = jnp.concatenate([part[-1]] * (WIDE // LANES), axis=1)
+        valid = jnp.sum(jnp.where(chosen, fills, 0.0), axis=0, keepdims=True)
         found.append((jnp.sum(jnp.where(chosen, values, 0.0), axis=0, keepdims=True), valid))
     partial_packet, fill_packet = (jnp.concatenate(x, axis=1) for x in zip(*found))
     image = jnp.sum(packet * pick(own[0:16, 0:bands], band), axis=0, keepdims=True)
@@ -396,7 +400,7 @@
         moved += [lax.ppermute(knot_coeffs, "tm", shifted), lax.ppermute(band_start, "tm", shifted)]
 
     send = send.reshape(devices * BLOCK, 1, LANES)
-    recv = lax.all_to_all(send, ("src", "tm"), split_axis=0, concat_axis=0, tiled=True)
+    recv = lax.all_to_all(send, ("tm", "src"), split_axis=0, concat_axis=0, tiled=True)
     recv = recv.reshape(devices * BLOCK, LANES)
     raw, gradient_source, gradient_knot, sums = pl.pallas_call(
         functools.partial(middle_kernel, groups, slabs),
@@ -423,7 +427,7 @@
         band_start,
         *moved,
     )
-    sums = lax.all_to_all(sums, ("src", "tm"), split_axis=0, concat_axis=0, tiled=True)
+    sums = lax.all_to_all(sums, ("tm", "src"), split_axis=0, concat_axis=0, tiled=True)
     like = [shape(x.shape, F32) for x in (left_vector, source_vector, knot_vector)]
     outs = pl.pallas_call(
         functools.partial(after_kernel, total_obs, unknowns),

time: 31.3 us -> 31.1 us (level)
  waiting for transfers between devices: 8.08 us -> 7.5 us
  blocking collectives: 9.13 us -> 9.5 us
    all_to_all x1, waiting for transfers between devices: 4.72 us -> 4.15 us  [shards(): lax.all_to_all(send, ('tm', 'src'), split_axis=0, concat_axis=0, tiled=True)]
    all_to_all x1, blocking collectives: 9.13 us -> 9.5 us  [shards(): lax.all_to_all(sums, ('tm', 'src'), split_axis=0, concat_axis=0, tiled=True)]
where the time goes in v5:
time: 31.1 us; the launch traced here: 30.8 us
  blocking collectives  9.5 us (31%)
  starting transfers between devices  9.39 us (30%)
  waiting for transfers between devices  7.5 us (24%)
  Pallas kernels  3.8 us (12%)
  between operations  0.66 us (2%)
    all_to_all x1, blocking collectives, shards(): lax.all_to_all(sums, ('tm', 'src'), split_axis=0, concat_axis=0, tiled=True)  9.5 us
    all_to_all x1, starting transfers between devices, shards(): lax.all_to_all(send, ('tm', 'src'), split_axis=0, concat_axis=0, tiled=True)  7.3 us
    all_to_all x1, waiting for transfers between devices, shards(): lax.all_to_all(send, ('tm', 'src'), split_axis=0, concat_axis=0, tiled=True)  4.15 us
    ppermute x1, waiting for transfers between devices, shards(): lax.ppermute(band_start, 'tm', shifted)  3.35 us
    pallas_call x1, Pallas kernels, shards(): pl.pallas_call(functools.partial(before_kernel, groups, slabs), out_shape...  2.18 us
    ppermute x1, starting transfers between devices, shards(): lax.ppermute(knot_coeffs, 'tm', shifted)  1.83 us
    pallas_call x1, Pallas kernels, shards(): pl.pallas_call(functools.partial(after_kernel, total_obs, unknowns), out_...  0.85 us
    pallas_call x1, Pallas kernels, shards(): pl.pallas_call(functools.partial(middle_kernel, groups, slabs), out_shape...  0.77 us
  transfers between devices with their start and end apart: 3, of which 2 were waited for; matrix products, arithmetic and copies ran while one was open for 0% of the time, Pallas kernels for 0%

profile of v5, /device:TPU:0, one launch (start us, length us, event | category | flops | bytes accessed | tf_op | source)
XLA Modules:
  0.0 30.8 jit_solution(16222354064750017168)
XLA Ops:
  0.6 2.2 %before.1 = (f32[448,128]{1,0:T(8,128)}, f32[2,256]{1,0:T(2,128)S(1)}, f32[24,128]{1,0:T(8,128)S(1)}, s32[2,256]{1,0:T(2,128)S(1)}, f32[5,2,256]{2,1,0:T(2,128)S...) custom-call(s32[2,256]{1,0:T(2,128)} %refs_0_.1, ...), custom_call_target="tpu_custom_call" | custom-call | tf_op jit(solution)/shard_map/before/pallas_call | solution.py:381
  2.8 7.3 %all-to-all-start = ((f32[448,1,128]{2,1,0:T(1,128)}), f32[448,1,128]{2,1,0:T(1,128)S(1)}, u32[]{:S(2)}, u32[]{:S(2)}) async-start(f32[448,1,128]{2,1,0:T(1,128)} %bitcast.2), calls=%async_computation | async-start | bytes 458752 | tf_op jit(solution)/shard_map/all_to_all | solution.py:403
  10.1 1.8 %collective-permute-start = (f32[12,2,256]{2,1,0:T(2,128)S(1)}, f32[12,2,256]{2,1,0:T(2,128)S(1)}, u32[]{:S(2)}, u32[]{:S(2)}) collective-permute-start(f32[12,2,256]{2,1,0:T(2,128)S(1)} %get-tuple-element.34.refs_0_), channel_id=1, source_target_pairs={{0,1},{1,0},{2,3},{3,2},{4,5},{5,4},{6,7},{7,6},{8,9},{9,8},{10,11... | collective-permute-start | bytes 73736 | tf_op jit(solution)/shard_map/ppermute | solution.py:400
  12.0 0.3 collective-permute-start.1
  12.2 3.4 %collective-permute-done.1.refs_3_ = s32[2,256]{1,0:T(2,128)S(1)} collective-permute-done((s32[2,256]{1,0:T(2,128)S(1)}, s32[2,256]{1,0:T(2,128)S(1)}, u32[]{:S(2)}, u32[]{:S(2)}) %collective-permute-start.1) | collective-permute-done | bytes 2080 | tf_op jit(solution)/shard_map/ppermute | solution.py:400
  15.6 0.0 collective-permute-done.refs_2_
  15.6 4.1 %all-to-all-done = f32[448,1,128]{2,1,0:T(1,128)S(1)} async-done(((f32[448,1,128]{2,1,0:T(1,128)}), f32[448,1,128]{2,1,0:T(1,128)S(1)}, u32[]{:S(2)}, u32[]{:S(2)}) %all-to-all-start) | async-done | bytes 229408 | tf_op jit(solution)/shard_map/all_to_all | solution.py:403
  19.7 0.8 %middle.1 = (f32[2,256]{1,0:T(2,128)S(1)}, f32[5,1024]{1,0:T(8,128)S(1)}, f32[3,1,256]{2,1,0:T(1,128)S(1)}, f32[32,128]{1,0:T(8,128)S(1)}) custom-call(f32[448,128]{1,0:T(8,128)S(1)} %bitcast.9, f32[2,256]{1,0:T(2,128)S(1)} %get-tuple-element.27.partial, f32[2,256]{1,0:T(2,128)S(1)} %get-tuple-element.28.left, s32[2,256]{1,0:T(2,128)S(1)} %get-tuple-element.29.source_index, ...), custom_call_target="tpu_custom_call" | custom-call | tf_op jit(solution)/shard_map/middle/pallas_call | solution.py:405
  20.5 9.5 %all_to_all.16 = f32[32,1,128]{2,1,0:T(1,128)S(1)} all-to-all(f32[32,1,128]{2,1,0:T(1,128)S(1)} %bitcast.11), channel_id=1, replica_groups=mesh['src'=16,'tm'=2] {'tm','src'}, dimensions={0} | all-to-all | bytes 32768 | tf_op jit(solution)/shard_map/all_to_all | solution.py:430
  30.0 0.8 %after.1 = (f32[2,256]{1,0:T(2,128)}, f32[5,1024]{1,0:T(8,128)}, f32[3,1,256]{2,1,0:T(1,128)}, f32[5,1024]{1,0:T(8,128)}, f32[3,1,256]{2,1,0:T(1,128)}, /*index=...) custom-call(f32[32,128]{1,0:T(8,128)S(1)} %bitcast.10, f32[24,128]{1,0:T(8,128)S(1)} %get-tuple-element.33.own, ...), custom_call_target="tpu_custom_call" | custom-call | tf_op jit(solution)/shard_map/after/pallas_call | solution.py:432
Async XLA Ops:
  2.8 16.9 %all-to-all-start = ((f32[448,1,128]{2,1,0:T(1,128)}), f32[448,1,128]{2,1,0:T(1,128)S(1)}, u32[]{:S(2)}, u32[]{:S(2)}) async-start(f32[448,1,128]{2,1,0:T(1,128)} %bitcast.2), calls=%async_computation | async-start | bytes 458752 | tf_op jit(solution)/shard_map/all_to_all | solution.py:403
  10.1 5.4 %collective-permute-start = (f32[12,2,256]{2,1,0:T(2,128)S(1)}, f32[12,2,256]{2,1,0:T(2,128)S(1)}, u32[]{:S(2)}, u32[]{:S(2)}) collective-permute-start(f32[12,2,256]{2,1,0:T(2,128)S(1)} %get-tuple-element.34.refs_0_), channel_id=1, source_target_pairs={{0,1},{1,0},{2,3},{3,2},{4,5},{5,4},{6,7},{7,6},{8,9},{9,8},{10,11... | collective-permute-start | bytes 73736 | tf_op jit(solution)/shard_map/ppermute | solution.py:400
  12.0 3.6 %collective-permute-start.1 = (s32[2,256]{1,0:T(2,128)S(1)}, s32[2,256]{1,0:T(2,128)S(1)}, u32[]{:S(2)}, u32[]{:S(2)}) collective-permute-start(s32[2,256]{1,0:T(2,128)S(1)} %get-tuple-element.35.refs_1_), channel_id=1, source_target_pairs={{0,1},{1,0},{2,3},{3,2},{4,5},{5,4},{6,7},{7,6},{8,9},{9,8},{10,11... | collective-permute-start | bytes 6152 | tf_op jit(solution)/shard_map/ppermute | solution.py:400
